TPU v7x, 512 devices: a whole 4x8x8 slice. The times are simulated.
512 devices in a mesh: lon: 32 (over y_lo, x, core), lat: 16 (over z, y_hi).
Axes of the slice: x: 4, y: 8 (y_hi: 2, y_lo: 4; y = y_hi * 4 + y_lo), z: 8, core: 2. Of those that a mesh axis runs over, the one named last changes fastest.
Arguments:
- fields: bfloat16 [128, 1024, 256], P('lat', 'lon'), may hold values from -6 to 6
- norm_lon: float32 [256], replicated, may hold values from 0.25 to 1.75
- query_lon: bfloat16 [256, 256], replicated, may hold values from -0.375 to 0.375
- key_lon: bfloat16 [256, 256], replicated, may hold values from -0.375 to 0.375
- value_lon: bfloat16 [256, 256], replicated, may hold values from -0.375 to 0.375
- out_lon: bfloat16 [256, 256], replicated, may hold values from -0.375 to 0.375
- temp_lon: float32 [8], replicated, may hold values from 0.5 to 12
- bias_lon: float32 [8], replicated, may hold values from -2 to 2
- norm_lat: float32 [256], replicated, may hold values from 0.25 to 1.75
- query_lat: bfloat16 [256, 256], replicated, may hold values from -0.375 to 0.375
- key_lat: bfloat16 [256, 256], replicated, may hold values from -0.375 to 0.375
- value_lat: bfloat16 [256, 256], replicated, may hold values from -0.375 to 0.375
- out_lat: bfloat16 [256, 256], replicated, may hold values from -0.375 to 0.375
- temp_lat: float32 [8], replicated, may hold values from 0.5 to 12
- bias_lat: float32 [8], replicated, may hold values from -4 to 0
- norm_mlp: float32 [256], replicated, may hold values from 0.25 to 1.75
- w_gate: bfloat16 [256, 1024], replicated, may hold values from -0.375 to 0.375
- w_up: bfloat16 [256, 1024], replicated, may hold values from -0.375 to 0.375
- w_down: bfloat16 [1024, 256], replicated, may hold values from -0.1875 to 0.1875
Outputs:
- updated: bfloat16 [128, 1024, 256], P('lat', 'lon')
All inputs are finite; a program needn't handle non-finite values.
Results may differ from a plain program's by a relative error of at most 0.018.
The roundings to bfloat16 on the way count: a program that leaves them out, or rounds other values in their place, can miss the bound.
Values may be sent and summed in bfloat16 or wider, within the bound.
No kernel may reach another device: no remote copies, remote signals or barrier semaphores. Data moves between devices by JAX's collectives and lax.ppermute only.
A program may use at most 64 MiB of HBM per device.

v0:
```python
import math

import jax
import jax.numpy as jnp
from jax import lax
from jax.sharding import PartitionSpec as P


def sent_together(arrays, axis, split_dim, concat_dim, along):
    widths = [a.shape[along] for a in arrays]
    both = jnp.concatenate(arrays, axis=along)
    out = lax.all_to_all(both, axis, split_axis=split_dim, concat_axis=concat_dim, tiled=True)
    return tuple(jnp.split(out, [sum(widths[:k]) for k in range(1, len(widths))], axis=along))


def normalize(values, gain):
    factor = lax.rsqrt(jnp.mean(values * values, axis=-1, keepdims=True) + 1e-06)
    return (values * factor * gain).astype(jnp.bfloat16)


def project(values, weight):
    return jnp.dot(values, weight, preferred_element_type=jnp.float32).astype(jnp.bfloat16)


def attend_lat(queries, keys, values, temp, bias):
    count, cols, depth = queries.shape
    heads = temp.shape[0]
    size = depth // heads
    qh = queries.reshape(count, cols, heads, size)
    kh = keys.reshape(count, cols, heads, size)
    vh = values.reshape(count, cols, heads, size)
    scores = jnp.einsum("ichd,jchd->chij", qh, kh, preferred_element_type=jnp.float32)
    place = jnp.arange(count, dtype=jnp.int32)
    spread = jnp.abs(place[:, None] - place[None, :]).astype(jnp.float32) / count
    scores = (
        scores * (temp / math.sqrt(size))[None, :, None, None]
        + bias[None, :, None, None] * spread[None, None]
    )
    expo = jnp.exp(scores - jnp.max(scores, axis=-1, keepdims=True))
    denom = jnp.sum(expo, axis=-1)
    mixed = jnp.einsum(
        "chij,jchd->ichd", expo.astype(jnp.bfloat16), vh, preferred_element_type=jnp.float32
    )
    mixed = mixed / jnp.transpose(denom, (2, 0, 1))[..., None]
    return mixed.astype(jnp.bfloat16).reshape(count, cols, depth)


def body(
    fields,
    norm_lon,
    query_lon,
    key_lon,
    value_lon,
    out_lon,
    temp_lon,
    bias_lon,
    norm_lat,
    query_lat,
    key_lat,
    value_lat,
    out_lat,
    temp_lat,
    bias_lat,
    norm_mlp,
    w_gate,
    w_up,
    w_down,
):
    rows, width, depth = fields.shape
    heads = temp_lon.shape[0]
    size = depth // heads
    total_lon = width * lax.axis_size("lon")
    resid = fields.astype(jnp.float32)
    normed = normalize(resid, norm_lon)
    scale_lon = temp_lon / math.sqrt(size)

    def by_problem(values_in):
        split_heads = values_in.reshape(rows, width, heads, size)
        return jnp.transpose(split_heads, (0, 2, 1, 3)).reshape(rows * heads, width, size)

    q_all, k_all, v_all = sent_together(
        (
            by_problem(project(normed, query_lon)),
            by_problem(project(normed, key_lon)),
            by_problem(project(normed, value_lon)),
        ),
        "lon",
        0,
        1,
        2,
    )
    owned = q_all.shape[0]
    problem = lax.axis_index("lon") * owned + jnp.arange(owned, dtype=jnp.int32)
    picker = (problem[:, None] % heads == jnp.arange(heads, dtype=jnp.int32)[None, :]).astype(
        jnp.float32
    )
    scale_own = jnp.sum(picker * scale_lon[None, :], axis=1)
    bias_own = jnp.sum(picker * bias_lon[None, :], axis=1)
    block = math.gcd(total_lon, 512)
    nblocks = total_lon // block
    key_place = jnp.arange(total_lon, dtype=jnp.int32)

    def one_problem(items):
        query_one, key_one, value_one, scale_one, bias_one = items
        query_blocks = query_one.reshape(nblocks, block, size)
        starts = jnp.arange(nblocks, dtype=jnp.int32) * block

        def one_block(pair):
            query_block, start = pair
            query_place = start + jnp.arange(block, dtype=jnp.int32)
            angle = (query_place[:, None] - key_place[None, :]).astype(jnp.float32) * (
                2.0 * math.pi / total_lon
            )
            scores = jnp.dot(query_block, key_one.T, preferred_element_type=jnp.float32)
            scores = scores * scale_one + bias_one * jnp.cos(angle)
            expo = jnp.exp(scores - jnp.max(scores, axis=-1, keepdims=True))
            denom = jnp.sum(expo, axis=-1)
            mixed = jnp.dot(
                expo.astype(jnp.bfloat16), value_one, preferred_element_type=jnp.float32
            )
            return (mixed / denom[:, None]).astype(jnp.bfloat16)

        return lax.map(one_block, (query_blocks, starts)).reshape(total_lon, size)

    solved = lax.map(one_problem, (q_all, k_all, v_all, scale_own, bias_own))
    back = lax.all_to_all(solved, "lon", split_axis=1, concat_axis=0, tiled=True)
    attended = jnp.transpose(back.reshape(rows, heads, width, size), (0, 2, 1, 3)).reshape(
        rows, width, depth
    )
    first = resid + jnp.dot(attended, out_lon, preferred_element_type=jnp.float32)
    normed_lat = normalize(first, norm_lat)
    moved = lax.all_to_all(normed_lat, "lat", split_axis=1, concat_axis=0, tiled=True)
    query_col = project(moved, query_lat)
    key_col = project(moved, key_lat)
    value_col = project(moved, value_lat)
    mixed_lat = attend_lat(query_col, key_col, value_col, temp_lat, bias_lat)
    returned = lax.all_to_all(mixed_lat, "lat", split_axis=0, concat_axis=1, tiled=True)
    second = first + jnp.dot(returned, out_lat, preferred_element_type=jnp.float32)
    normed_mlp = normalize(second, norm_mlp)
    gate = jnp.dot(normed_mlp, w_gate, preferred_element_type=jnp.float32)
    upper = jnp.dot(normed_mlp, w_up, preferred_element_type=jnp.float32)
    hidden = (jax.nn.silu(gate) * upper).astype(jnp.bfloat16)
    return (second + jnp.dot(hidden, w_down, preferred_element_type=jnp.float32)).astype(
        jnp.bfloat16
    )


def solution(mesh):
    in_specs = (
        P("lat", "lon", None),
        P(),
        P(),
        P(),
        P(),
        P(),
        P(),
        P(),
        P(),
        P(),
        P(),
        P(),
        P(),
        P(),
        P(),
        P(),
        P(),
        P(),
        P(),
    )
    out_specs = P("lat", "lon", None)
    return jax.shard_map(body, mesh=mesh, in_specs=in_specs, out_specs=out_specs, check_vma=False)
```

profile of v0, /device:TPU:8, one launch (start us, length us, event | category | flops | bytes accessed | tf_op | source)
XLA Modules:
  0.0 142.0 jit_solution(2078558824579664427)
XLA Ops:
  0.0 1.1 fusion.34
  1.1 1.2 convolution_convert_fusion.3
  4.0 1.3 pad_maximum_fusion
  5.2 9.4 %all-to-all-start = ((bf16[64,32,96]{2,1,0:T(8,128)(2,1)}), bf16[64,32,96]{2,1,0:T(8,128)(2,1)S(1)}, u32[]{:S(2)}, u32[]{:S(2)}) async-start(bf16[64,32,96]{2,1,0:T(8,128)(2,1)} %pad_maximum_fusion), calls=%async_computation | async-start | bytes 1048576 | tf_op jit(solution)/shard_map/all_to_all | solution.py:12
  14.9 15.2 %all-to-all-done = bf16[64,32,96]{2,1,0:T(8,128)(2,1)S(1)} async-done(((bf16[64,32,96]{2,1,0:T(8,128)(2,1)}), bf16[64,32,96]{2,1,0:T(8,128)(2,1)S(1)}, u32[]{:S(2)}, u32[]{:S(2)}) %all-to-all-start) | async-done | bytes 393248 | tf_op jit(solution)/shard_map/all_to_all | solution.py:12
  30.1 0.3 fusion.63
  30.5 48.0 %while.23 = (s32[]{:T(128)}, bf16[2,1024,32]{2,1,0:T(8,128)(2,1)}, bf16[2,1024,32]{2,1,0:T(8,128)(2,1)S(1)}, bf16[2,1024,32]{2,1,0:T(8,128)(2,1)S(1)}, f32[2]{0:...) while((s32[]{:T(128)}, bf16[2,1024,32]{2,1,0:T(8,128)(2,1)}, ...), condition=%wide.region_8.9_spmd.clone, body=%wide.region_3.8_spmd.clone.sunk | while | flops 72908288 | bytes 7854954 | solution.py:125
  30.6 0.6 dynamic_slice.47
  31.1 0.6 dynamic_slice.48
  31.7 21.8 %while.24 = (s32[]{:T(128)}, bf16[2,512,32]{1,2,0:T(8,128)(2,1)S(1)}, bf16[2,512,32]{2,1,0:T(8,128)(2,1)S(1)}, bf16[1024,32]{1,0:T(8,128)(2,1)S(1)}, f32[]{:T(12...) while((s32[]{:T(128)}, ...), condition=%wide.region_7.7_spmd, body=%wide.region_4.6_spmd.sunk | while | flops 72908288 | bytes 6998149 | solution.py:123
  31.7 0.6 dynamic_slice.50
  32.4 0.6 iota_add_fusion.2
  33.0 8.6 %fusion.81 = (f32[512]{0:T(512)S(1)}, f32[512,1024]{1,0:T(8,128)S(1)}) fusion(s32[1024]{0:T(1024)S(1)} %get-tuple-element.313, s32[512]{0:T(512)S(1)} %iota_add_fusion.2, f32[]{:T(128)} %get-tuple-element.311, f32[]{:T(128)} %get-tuple-element.310, bf16[1024,32]{1,0:T(8,128)(2,1)S(1)} %get-tuple-element.309, ...), kind=kOutput, calls=%fused_computation.95.clone.1 | convolution fusion | flops 37223936 | bytes 2498572 | tf_op jit(solution)/shard_map/while/body/eval_jaxpr/while/body/eval_jaxpr/dot_general | solution.py:114
  41.6 0.5 fusion.82
  42.2 0.5 fusion.83
  42.7 0.6 dynamic_slice.50
  43.3 0.6 iota_add_fusion.2
  43.9 8.6 %fusion.81 = (f32[512]{0:T(512)S(1)}, f32[512,1024]{1,0:T(8,128)S(1)}) fusion(s32[1024]{0:T(1024)S(1)} %get-tuple-element.313, s32[512]{0:T(512)S(1)} %iota_add_fusion.2, f32[]{:T(128)} %get-tuple-element.311, f32[]{:T(128)} %get-tuple-element.310, bf16[1024,32]{1,0:T(8,128)(2,1)S(1)} %get-tuple-element.309, ...), kind=kOutput, calls=%fused_computation.95.clone.1 | convolution fusion | flops 37223936 | bytes 2498572 | tf_op jit(solution)/shard_map/while/body/eval_jaxpr/while/body/eval_jaxpr/dot_general | solution.py:114
  52.6 0.5 fusion.82
  53.1 0.5 fusion.83
  53.8 0.7 bitcast_dynamic-update-slice_fusion.2
  54.6 0.6 dynamic_slice.47
  55.2 0.6 dynamic_slice.48
  55.8 21.8 %while.24 = (s32[]{:T(128)}, bf16[2,512,32]{1,2,0:T(8,128)(2,1)S(1)}, bf16[2,512,32]{2,1,0:T(8,128)(2,1)S(1)}, bf16[1024,32]{1,0:T(8,128)(2,1)S(1)}, f32[]{:T(12...) while((s32[]{:T(128)}, ...), condition=%wide.region_7.7_spmd, body=%wide.region_4.6_spmd.sunk | while | flops 72908288 | bytes 6998149 | solution.py:123
  55.8 0.6 dynamic_slice.50
  56.4 0.6 iota_add_fusion.2
  57.0 8.6 %fusion.81 = (f32[512]{0:T(512)S(1)}, f32[512,1024]{1,0:T(8,128)S(1)}) fusion(s32[1024]{0:T(1024)S(1)} %get-tuple-element.313, s32[512]{0:T(512)S(1)} %iota_add_fusion.2, f32[]{:T(128)} %get-tuple-element.311, f32[]{:T(128)} %get-tuple-element.310, bf16[1024,32]{1,0:T(8,128)(2,1)S(1)} %get-tuple-element.309, ...), kind=kOutput, calls=%fused_computation.95.clone.1 | convolution fusion | flops 37223936 | bytes 2498572 | tf_op jit(solution)/shard_map/while/body/eval_jaxpr/while/body/eval_jaxpr/dot_general | solution.py:114
  65.6 0.5 fusion.82
  66.2 0.5 fusion.83
  66.7 0.6 dynamic_slice.50
  67.3 0.6 iota_add_fusion.2
  67.9 8.6 %fusion.81 = (f32[512]{0:T(512)S(1)}, f32[512,1024]{1,0:T(8,128)S(1)}) fusion(s32[1024]{0:T(1024)S(1)} %get-tuple-element.313, s32[512]{0:T(512)S(1)} %iota_add_fusion.2, f32[]{:T(128)} %get-tuple-element.311, f32[]{:T(128)} %get-tuple-element.310, bf16[1024,32]{1,0:T(8,128)(2,1)S(1)} %get-tuple-element.309, ...), kind=kOutput, calls=%fused_computation.95.clone.1 | convolution fusion | flops 37223936 | bytes 2498572 | tf_op jit(solution)/shard_map/while/body/eval_jaxpr/while/body/eval_jaxpr/dot_general | solution.py:114
  76.6 0.5 fusion.82
  77.1 0.5 fusion.83
  77.8 0.7 bitcast_dynamic-update-slice_fusion.2
  78.5 1.6 %copy.108 = bf16[2,1024,32]{2,0,1:T(2,128)(2,1)S(1)} copy(bf16[2,1024,32]{2,1,0:T(8,128)(2,1)} %get-tuple-element.94) | data formatting | bytes 262144 | tf_op jit(solution)/shard_map/while | solution.py:125
  80.1 1.2 reshape.149
  81.3 5.1 %all-to-all-start.1 = ((bf16[32,2,1024]{2,1,0:T(2,128)(2,1)}), bf16[32,2,1024]{2,1,0:T(2,128)(2,1)S(1)}, u32[]{:S(2)}, u32[]{:S(2)}) async-start(bf16[32,2,1024]{2,1,0:T(2,128)(2,1)} %reshape.149), calls=%async_computation.1 | async-start | bytes 262144 | tf_op jit(solution)/shard_map/all_to_all | solution.py:126
  86.4 7.4 %all-to-all-done.1 = bf16[32,2,1024]{2,1,0:T(2,128)(2,1)S(1)} async-done(((bf16[32,2,1024]{2,1,0:T(2,128)(2,1)}), bf16[32,2,1024]{2,1,0:T(2,128)(2,1)S(1)}, u32[]{:S(2)}, u32[]{:S(2)}) %all-to-all-start.1) | async-done | bytes 131104 | tf_op jit(solution)/shard_map/all_to_all | solution.py:126
  94.4 0.4 reshape.132
  94.8 0.3 multiply_reduce_fusion.1
  95.2 0.7 copy.81
  95.9 11.8 %all-to-all-start.2 = ((bf16[8,32,256]{2,0,1:T(8,128)(2,1)}), bf16[8,32,256]{2,0,1:T(8,128)(2,1)S(1)}, u32[]{:S(2)}, u32[]{:S(2)}) async-start(bf16[8,32,256]{2,0,1:T(8,128)(2,1)} %copy.81), calls=%async_computation.2 | async-start | bytes 262144 | tf_op jit(solution)/shard_map/all_to_all | solution.py:132
  107.9 13.8 %all-to-all-done.2 = bf16[8,32,256]{2,0,1:T(8,128)(2,1)S(1)} async-done(((bf16[8,32,256]{2,0,1:T(8,128)(2,1)}), bf16[8,32,256]{2,0,1:T(8,128)(2,1)S(1)}, u32[]{:S(2)}, u32[]{:S(2)}) %all-to-all-start.2) | async-done | bytes 131104 | tf_op jit(solution)/shard_map/all_to_all | solution.py:132
  122.6 0.4 fusion.64
  123.6 16.2 %all_to_all.69 = bf16[128,2,256]{2,1,0:T(2,128)(2,1)S(1)} all-to-all(bf16[128,2,256]{2,1,0:T(2,128)(2,1)S(1)} %copy.87), channel_id=1, replica_groups=mesh['lon'=32,'lat'=16] {'lat'}, dimensions={0} | all-to-all | bytes 262144 | tf_op jit(solution)/shard_map/all_to_all | solution.py:137
  140.4 0.3 fusion.30
  140.7 1.3 fusion.18
  (84 shorter events, 5.0 us)
Async XLA Ops:
  0.0 140.3 %copy-start = (bf16[256,1024]{1,0:T(8,128)(2,1)S(1)}, bf16[256,1024]{1,0:T(8,128)(2,1)}, u32[]{:S(2)}) copy-start(bf16[256,1024]{1,0:T(8,128)(2,1)} %param.39) | copy-start | bytes 1572868
  0.0 2.7 %copy-start.1 = (bf16[8,32,256]{2,1,0:T(8,128)(2,1)S(1)}, bf16[8,32,256]{2,1,0:T(8,128)(2,1)}, u32[]{:S(2)}) copy-start(bf16[8,32,256]{2,1,0:T(8,128)(2,1)} %param.23) | copy-start | bytes 393220
  0.0 2.7 %copy-start.9 = (f32[256]{0:T(256)S(1)}, f32[256]{0:T(256)}, u32[]{:S(2)}) copy-start(f32[256]{0:T(256)} %param.24) | copy-start | bytes 3076
  0.0 2.7 %copy-start.2 = (bf16[256,256]{1,0:T(8,128)(2,1)S(1)}, bf16[256,256]{1,0:T(8,128)(2,1)}, u32[]{:S(2)}) copy-start(bf16[256,256]{1,0:T(8,128)(2,1)} %param.25) | copy-start | bytes 393220
  1.1 2.2 %copy-start.3 = (bf16[256,256]{1,0:T(8,128)(2,1)S(1)}, bf16[256,256]{1,0:T(8,128)(2,1)}, u32[]{:S(2)}) copy-start(bf16[256,256]{1,0:T(8,128)(2,1)} %param.26) | copy-start | bytes 393220
  3.8 10.9 %copy-start.16 = (f32[8]{0:T(128)S(1)}, f32[8]{0:T(128)}, u32[]{:S(2)}) copy-start(f32[8]{0:T(128)} %param.29) | copy-start | bytes 100
  3.8 10.9 %copy-start.12 = (f32[8]{0:T(128)S(1)}, f32[8]{0:T(128)}, u32[]{:S(2)}) copy-start(f32[8]{0:T(128)} %param.30) | copy-start | bytes 100
  5.2 24.8 %all-to-all-start = ((bf16[64,32,96]{2,1,0:T(8,128)(2,1)}), bf16[64,32,96]{2,1,0:T(8,128)(2,1)S(1)}, u32[]{:S(2)}, u32[]{:S(2)}) async-start(bf16[64,32,96]{2,1,0:T(8,128)(2,1)} %pad_maximum_fusion), calls=%async_computation | async-start | bytes 1048576 | tf_op jit(solution)/shard_map/all_to_all | solution.py:12
  30.5 55.9 %copy-start.17 = (f32[8]{0:T(128)S(1)}, f32[8]{0:T(128)}, u32[]{:S(2)}) copy-start(f32[8]{0:T(128)} %param.36) | copy-start | bytes 100
  80.1 14.7 %copy-start.4 = (bf16[256,256]{1,0:T(8,128)(2,1)S(1)}, bf16[256,256]{1,0:T(8,128)(2,1)}, u32[]{:S(2)}) copy-start(bf16[256,256]{1,0:T(8,128)(2,1)} %param.28) | copy-start | bytes 393220
  81.3 12.5 %all-to-all-start.1 = ((bf16[32,2,1024]{2,1,0:T(2,128)(2,1)}), bf16[32,2,1024]{2,1,0:T(2,128)(2,1)S(1)}, u32[]{:S(2)}, u32[]{:S(2)}) async-start(bf16[32,2,1024]{2,1,0:T(2,128)(2,1)} %reshape.149), calls=%async_computation.1 | async-start | bytes 262144 | tf_op jit(solution)/shard_map/all_to_all | solution.py:126
  86.4 8.7 %copy-start.10 = (f32[256]{0:T(256)S(1)}, f32[256]{0:T(256)}, u32[]{:S(2)}) copy-start(f32[256]{0:T(256)} %param.31) | copy-start | bytes 3076
  94.1 13.7 %copy-start.13 = (f32[8]{0:T(128)S(1)}, f32[8]{0:T(128)}, u32[]{:S(2)}) copy-start(f32[8]{0:T(128)} %param.37) | copy-start | bytes 100
  94.2 27.5 %copy-start.5 = (bf16[256,256]{1,0:T(8,128)(2,1)S(1)}, bf16[256,256]{1,0:T(8,128)(2,1)}, u32[]{:S(2)}) copy-start(bf16[256,256]{1,0:T(8,128)(2,1)} %param.32) | copy-start | bytes 393220
  94.2 27.8 %copy-start.6 = (bf16[256,256]{1,0:T(8,128)(2,1)S(1)}, bf16[256,256]{1,0:T(8,128)(2,1)}, u32[]{:S(2)}) copy-start(bf16[256,256]{1,0:T(8,128)(2,1)} %param.33) | copy-start | bytes 393220
  94.4 27.9 %copy-start.7 = (bf16[256,256]{1,0:T(8,128)(2,1)S(1)}, bf16[256,256]{1,0:T(8,128)(2,1)}, u32[]{:S(2)}) copy-start(bf16[256,256]{1,0:T(8,128)(2,1)} %param.34) | copy-start | bytes 393220
  95.9 25.7 %all-to-all-start.2 = ((bf16[8,32,256]{2,0,1:T(8,128)(2,1)}), bf16[8,32,256]{2,0,1:T(8,128)(2,1)S(1)}, u32[]{:S(2)}, u32[]{:S(2)}) async-start(bf16[8,32,256]{2,0,1:T(8,128)(2,1)} %copy.81), calls=%async_computation.2 | async-start | bytes 262144 | tf_op jit(solution)/shard_map/all_to_all | solution.py:132
  123.0 17.0 %copy-start.8 = (bf16[256,256]{1,0:T(8,128)(2,1)S(1)}, bf16[256,256]{1,0:T(8,128)(2,1)}, u32[]{:S(2)}) copy-start(bf16[256,256]{1,0:T(8,128)(2,1)} %param.35) | copy-start | bytes 393220
  123.2 17.2 %copy-start.11 = (f32[256]{0:T(256)S(1)}, f32[256]{0:T(256)}, u32[]{:S(2)}) copy-start(f32[256]{0:T(256)} %param.38) | copy-start | bytes 3076
  123.5 17.2 %copy-start.14 = (bf16[1024,256]{1,0:T(8,128)(2,1)S(1)}, bf16[1024,256]{1,0:T(8,128)(2,1)}, u32[]{:S(2)}) copy-start(bf16[1024,256]{1,0:T(8,128)(2,1)} %param.41) | copy-start | bytes 1572868
  123.5 17.2 %copy-start.15 = (bf16[256,1024]{1,0:T(8,128)(2,1)S(1)}, bf16[256,1024]{1,0:T(8,128)(2,1)}, u32[]{:S(2)}) copy-start(bf16[256,1024]{1,0:T(8,128)(2,1)} %param.40) | copy-start | bytes 1572868
where the time goes:
time: 143 us; the launch traced here: 142 us
  matrix products  41.5 us (29%)
  waiting for transfers between devices  36.3 us (25%)
  starting transfers between devices  26.3 us (18%)
  blocking collectives  16.2 us (11%)
  local copies, waits for them, and re-layouts  13.4 us (9%)
  other arithmetic  7.53 us (5%)
    dot_general x4, matrix products, one_block(): scores = jnp.dot(query_block, key_one.T, preferred_element_type=jnp.float32)  34.5 us
    all_to_all x1, blocking collectives, body(): lax.all_to_all(mixed_lat, 'lat', split_axis=0, concat_axis=1, tiled=True)  16.2 us
    all_to_all x1, waiting for transfers between devices, sent_together(): lax.all_to_all(both, axis, split_axis=split_dim, concat_axis=concat_dim,...  15.2 us
    all_to_all x1, waiting for transfers between devices, body(): lax.all_to_all(normed_lat, 'lat', split_axis=1, concat_axis=0, tiled=True)  13.8 us
    all_to_all x1, starting transfers between devices, body(): lax.all_to_all(normed_lat, 'lat', split_axis=1, concat_axis=0, tiled=True)  11.8 us
    all_to_all x1, starting transfers between devices, sent_together(): lax.all_to_all(both, axis, split_axis=split_dim, concat_axis=concat_dim,...  9.41 us
    all_to_all x1, waiting for transfers between devices, body(): lax.all_to_all(solved, 'lon', split_axis=1, concat_axis=0, tiled=True)  7.37 us
    all_to_all x1, starting transfers between devices, body(): lax.all_to_all(solved, 'lon', split_axis=1, concat_axis=0, tiled=True)  5.11 us
  transfers between devices with their start and end apart: 3, of which 3 were waited for; matrix products, arithmetic and copies ran while one was open for 0% of the time, Pallas kernels for 0%

commit v1 on v0

v1 whole, which is shorter than its diff:
```python
import functools
import math

import jax
import jax.numpy as jnp
import numpy as np
from jax import lax
from jax.experimental import pallas as pl
from jax.experimental.pallas import tpu as pltpu
from jax.sharding import Mesh
from jax.sharding import PartitionSpec as P

YL, X, C, Z, YH = 4, 4, 2, 8, 2
HEADS, HEAD, D = 8, 32, 256
F32, BF16 = jnp.float32, jnp.bfloat16
LOG2E = 1.0 / math.log(2.0)
VMEM = pl.BlockSpec(memory_space=pltpu.VMEM)
SMEM = pl.BlockSpec(memory_space=pltpu.SMEM)
PARAMS = pltpu.CompilerParams(vmem_limit_bytes=40 * 1024 * 1024)


def dot(a, b):
    return jnp.dot(a, b, preferred_element_type=F32)


def normed(values, gain):
    factor = lax.rsqrt(jnp.mean(values * values, axis=-1, keepdims=True) + 1e-06)
    return (values * factor * gain).astype(BF16)


def row_kernel(
    yl_ref, ratio_ref, scale_ref, x_ref, gain_ref, wq_ref, wk_ref, wv_ref, wo_ref, keyf_ref, wave_ref,
    out_ref, norm_s, kext_s, att_s, first_s, send_s,
):
    own = pl.ds(pl.multiple_of(yl_ref[0] * 256, 256), 256)
    norm_s[...] = normed(x_ref[...].astype(F32), gain_ref[...])
    keys = dot(norm_s[...], wk_ref[...]).astype(BF16)
    for g in range(2):
        kext_s[g, :, :128] = keys[:, 128 * g : 128 * g + 128]
        kext_s[g, :, 128:] = keyf_ref[...]
    vals_t = dot(norm_s[...], wv_ref[...]).T.astype(BF16)
    qs_t = dot(norm_s[own, :], wq_ref[...]).T.astype(BF16)
    wave = wave_ref[:, own]
    low_rows = lax.broadcasted_iota(jnp.int32, wave.shape, 0) % 3 == 2
    ones = jnp.ones((16, 1024), BF16)
    for h in range(HEADS):
        at = HEAD * (h % 4)
        full = wave * ratio_ref[h]
        high = full.astype(BF16).astype(F32)
        feats = jnp.where(low_rows, full - high, high).astype(BF16)
        parts = [qs_t[HEAD * h : HEAD * h + HEAD], feats, jnp.zeros((112, 256), BF16)]
        if at + HEAD < 128:
            parts.insert(1, jnp.zeros((128 - at - HEAD, 256), BF16))
        if at:
            parts.insert(0, jnp.zeros((at, 256), BF16))
        scores = dot(kext_s[h // 4], jnp.concatenate(parts, axis=0))
        peak = jnp.max(scores, axis=0, keepdims=True)
        expo = jnp.exp2((scores - peak) * scale_ref[h]).astype(BF16)
        mixed = dot(jnp.concatenate([vals_t[HEAD * h : HEAD * h + HEAD], ones], axis=0), expo)
        att_s[HEAD * h : HEAD * h + HEAD, :] = mixed[:HEAD] / mixed[HEAD : HEAD + 1]
    attended = att_s[...].T.astype(BF16)
    first_s[...] = x_ref[own, :].astype(F32) + dot(attended, wo_ref[...])
    for xc in range(8):
        for k in range(4):
            rows = first_s[32 * xc + 8 * k : 32 * xc + 8 * k + 8, :]
            send_s[pl.ds(8 * xc + k, 8, stride=64), :] = rows[:, :128]
            send_s[pl.ds(8 * xc + 4 + k, 8, stride=64), :] = rows[:, 128:]
    sent = send_s[...].astype(BF16)
    out_ref[0] = sent
    out_ref[1] = sent


def col_kernel(
    yh_ref, scale_ref, slope_ref, x_ref, gain_ref, wq_ref, wk_ref, wv_ref, wo_ref, gain2_ref, wg_ref, wu_ref, wd_ref,
    out_ref, wide_s, first_s, norm_s,
):
    wide_s[...] = x_ref[...].astype(F32)
    for k in range(4):
        for f in range(2):
            first_s[k, :, 128 * f : 128 * f + 128] = wide_s[pl.ds(4 * f + k, 128, stride=8), :]
    for k in range(4):
        norm_s[k] = normed(first_s[k], gain_ref[...])
    own = pl.ds(pl.multiple_of(yh_ref[0] * 64, 64), 64)
    flat = norm_s[...].reshape(512, D)
    keys = dot(flat, wk_ref[...]).astype(BF16)
    vals = dot(flat, wv_ref[...]).astype(BF16)
    mine = jnp.concatenate([norm_s[k, own, :] for k in range(4)], axis=0)
    qs = dot(mine, wq_ref[...])
    a = lax.broadcasted_iota(jnp.int32, (64, 128), 0)
    b = lax.broadcasted_iota(jnp.int32, (64, 128), 1)
    lat_a = 16 * (a // 8) + 8 * yh_ref[0] + a % 8
    lat_b = 16 * ((b // 8) % 8) + 8 * (b // 64) + b % 8
    spread = jnp.abs(lat_a - lat_b).astype(F32) * (1.0 / 128)
    head_of = lax.broadcasted_iota(jnp.int32, (64, D), 1) // HEAD
    mixes = []
    for k in range(4):
        q_one = qs[64 * k : 64 * k + 64]
        masked = jnp.concatenate([jnp.where(head_of == h, q_one, 0.0) for h in range(HEADS)], axis=0).astype(BF16)
        raw = lax.dot_general(
            masked, keys[128 * k : 128 * k + 128], (((1,), (1,)), ((), ())), preferred_element_type=F32
        )
        scores = jnp.concatenate(
            [raw[64 * h : 64 * h + 64] * scale_ref[h] + spread * slope_ref[h] for h in range(HEADS)], axis=0
        )
        expo = jnp.exp2(scores - jnp.max(scores, axis=-1, keepdims=True))
        denom = jnp.sum(expo, axis=-1, keepdims=True)
        mixed = dot(expo.astype(BF16), vals[128 * k : 128 * k + 128]) / denom
        total = jnp.where(head_of == 0, mixed[:64], 0.0)
        for h in range(1, HEADS):
            total = jnp.where(head_of == h, mixed[64 * h : 64 * h + 64], total)
        mixes.append(total.astype(BF16))
    resid = jnp.concatenate([first_s[k, own, :] for k in range(4)], axis=0)
    second = resid + dot(jnp.concatenate(mixes, axis=0), wo_ref[...])
    third = normed(second, gain2_ref[...])
    gate = dot(third, wg_ref[...])
    upper = dot(third, wu_ref[...])
    hidden = (gate / (1.0 + jnp.exp(-gate)) * upper).astype(BF16)
    updated = second + dot(hidden, wd_ref[...])
    for k in range(4):
        for z in range(8):
            out_ref[z, k] = updated[64 * k + 8 * z : 64 * k + 8 * z + 8].astype(BF16)


def place_kernel(x_ref, out_ref, wide_s):
    wide_s[0] = x_ref[:, :128].astype(F32)
    wide_s[1] = x_ref[:, 128:].astype(F32)
    for row in range(8):
        parts = []
        for k in range(4):
            at = pl.ds(8 * k + row, 8, stride=32)
            parts.append(jnp.concatenate([wide_s[0, at, :], wide_s[1, at, :]], axis=1))
        out_ref[row] = jnp.concatenate(parts, axis=0).astype(BF16)


def tables():
    angle = np.arange(1024) * (2.0 * math.pi / 1024)
    cos, sin = np.cos(angle), np.sin(angle)
    wave = np.zeros((16, 1024), np.float32)
    wave[0:3], wave[3:6] = cos, sin
    keyf = np.zeros((1024, 128), np.float32)
    for at, v in ((0, cos), (3, sin)):
        high = v.astype(jnp.bfloat16).astype(np.float64)
        keyf[:, at], keyf[:, at + 1], keyf[:, at + 2] = high, v - high, high
    return keyf.astype(jnp.bfloat16), wave


def body(
    fields, norm_lon, query_lon, key_lon, value_lon, out_lon, temp_lon, bias_lon,
    norm_lat, query_lat, key_lat, value_lat, out_lat, temp_lat, bias_lat, norm_mlp, w_gate, w_up, w_down,
):
    keyf, wave = tables()
    yl = lax.axis_index("yl").astype(jnp.int32).reshape(1)
    yh = lax.axis_index("yh").astype(jnp.int32).reshape(1)
    scale_lon = temp_lon / math.sqrt(HEAD)
    scale_lat = temp_lat * (LOG2E / math.sqrt(HEAD))
    row = lax.all_to_all(
        jnp.concatenate([fields] * YL, axis=0), ("yl", "x", "c"), split_axis=0, concat_axis=0, tiled=True
    )
    sent = pl.pallas_call(
        row_kernel,
        out_shape=jax.ShapeDtypeStruct((2, 512, 128), BF16),
        in_specs=[SMEM] * 3 + [VMEM] * 8,
        out_specs=VMEM,
        scratch_shapes=[
            pltpu.VMEM((1024, D), BF16),
            pltpu.VMEM((2, 1024, D), BF16),
            pltpu.VMEM((D, 256), F32),
            pltpu.VMEM((256, D), F32),
            pltpu.VMEM((512, 128), F32),
        ],
        compiler_params=PARAMS,
    )(
        yl, bias_lon / scale_lon, scale_lon * LOG2E, row.reshape(1024, D), norm_lon.reshape(1, D),
        query_lon, key_lon, value_lon, out_lon, keyf, wave,
    )
    cols = lax.all_to_all(
        sent.reshape(128, 8, 128), ("yh", "z", "x", "c"), split_axis=0, concat_axis=0, tiled=True
    )
    done = pl.pallas_call(
        col_kernel,
        out_shape=jax.ShapeDtypeStruct((8, 4, 8, D), BF16),
        in_specs=[SMEM] * 3 + [VMEM] * 10,
        out_specs=VMEM,
        scratch_shapes=[
            pltpu.VMEM((1024, 128), F32),
            pltpu.VMEM((4, 128, D), F32),
            pltpu.VMEM((4, 128, D), BF16),
        ],
        compiler_params=PARAMS,
    )(
        yh, scale_lat, bias_lat * LOG2E, cols.reshape(1024, 128), norm_lat.reshape(1, D),
        query_lat, key_lat, value_lat, out_lat, norm_mlp.reshape(1, D), w_gate, w_up, w_down,
    )
    home = lax.all_to_all(done.reshape(8, 32, D), "z", split_axis=0, concat_axis=0, tiled=True)
    return pl.pallas_call(
        place_kernel,
        out_shape=jax.ShapeDtypeStruct((8, 32, D), BF16),
        in_specs=[VMEM],
        out_specs=VMEM,
        scratch_shapes=[pltpu.VMEM((2, 256, 128), F32)],
        compiler_params=PARAMS,
    )(home.reshape(256, D))


def solution(mesh):
    fine = Mesh(mesh.devices.reshape(YL, X, C, Z, YH), ("yl", "x", "c", "z", "yh"))
    cells = P(("z", "yh"), ("yl", "x", "c"), None)
    return jax.shard_map(body, mesh=fine, in_specs=(cells,) + (P(),) * 18, out_specs=cells, check_vma=False)
```

time: 143 us -> 85.1 us (0.60)
  matrix products: 41.5 us -> 0 us
  Pallas kernels: 0 us -> 11.5 us
  local copies, waits for them, and re-layouts: 13.4 us -> 2.63 us
  other arithmetic: 7.53 us -> 2.01 us
  blocking collectives: 16.2 us -> 12 us
  waiting for transfers between devices: 36.3 us -> 32.5 us
  starting transfers between devices: 26.3 us -> 23.9 us
    dot_general x20 -> x0, matrix products: 41.5 us -> none  [the longest x4 34.5 us: one_block(): scores = jnp.dot(query_block, key_one.T, preferred_element_type=jnp.float32)]
    pallas_call x0 -> x3, Pallas kernels: none -> 11.5 us  [the longest x1 7.91 us: body(): pl.pallas_call(row_kernel, out_shape=jax.ShapeDtypeStruct((2, 512, 128),...]
    dynamic_slice x10 -> x0, local copies, waits for them, and re-layouts: 4.96 us -> none  [the longest x4 2.56 us: one_problem(): return lax.map(one_block, (query_blocks, starts)).reshape(total_lon, size)]
    all_to_all x1, blocking collectives: 16.2 us -> 12 us  [body(): lax.all_to_all(done.reshape(8, 32, D), 'z', split_axis=0, concat_axis=0,...]
    all_to_all x3 -> x2, waiting for transfers between devices: 36.3 us -> 32.5 us  [the longest x1 17.7 us: body(): lax.all_to_all(sent.reshape(128, 8, 128), ('yh', 'z', 'x', 'c'), split_ax...]
    reduce_sum x7 -> x0, other arithmetic: 3.5 us -> none  [the longest x4 2.07 us: one_block(): denom = jnp.sum(expo, axis=-1)]
    add x4 -> x0, other arithmetic: 2.48 us -> none  [one_block(): query_place = start + jnp.arange(block, dtype=jnp.int32)]
    all_to_all x3 -> x2, starting transfers between devices: 26.3 us -> 23.9 us  [the longest x1 14.4 us: body(): lax.all_to_all(sent.reshape(128, 8, 128), ('yh', 'z', 'x', 'c'), split_ax...]
  transfers between devices with their start and end apart: 3 -> 2, of which waited for: 3 -> 2; matrix products, arithmetic and copies ran while one was open for 0% -> 0% of each run, Pallas kernels for 0% -> 0%
where the time goes in v1:
time: 85.1 us; the launch traced here: 84.7 us
  waiting for transfers between devices  32.5 us (38%)
  starting transfers between devices  23.9 us (28%)
  blocking collectives  12 us (14%)
  Pallas kernels  11.5 us (14%)
  local copies, waits for them, and re-layouts  2.63 us (3%)
  other arithmetic  2.01 us (2%)
    all_to_all x1, waiting for transfers between devices, body(): lax.all_to_all(sent.reshape(128, 8, 128), ('yh', 'z', 'x', 'c'), split_ax...  17.7 us
    all_to_all x1, waiting for transfers between devices, body(): lax.all_to_all(jnp.concatenate([fields] * YL, axis=0), ('yl', 'x', 'c'),...  14.7 us
    all_to_all x1, starting transfers between devices, body(): lax.all_to_all(sent.reshape(128, 8, 128), ('yh', 'z', 'x', 'c'), split_ax...  14.4 us
    all_to_all x1, blocking collectives, body(): lax.all_to_all(done.reshape(8, 32, D), 'z', split_axis=0, concat_axis=0,...  12 us
    all_to_all x1, starting transfers between devices, body(): lax.all_to_all(jnp.concatenate([fields] * YL, axis=0), ('yl', 'x', 'c'),...  9.56 us
    pallas_call x1, Pallas kernels, body(): pl.pallas_call(row_kernel, out_shape=jax.ShapeDtypeStruct((2, 512, 128),...  7.91 us
    pallas_call x1, Pallas kernels, body(): pl.pallas_call(col_kernel, out_shape=jax.ShapeDtypeStruct((8, 4, 8, D), B...  2.74 us
    unnamed x40, local copies, waits for them, and re-layouts  2.63 us
  transfers between devices with their start and end apart: 2, of which 2 were waited for; matrix products, arithmetic and copies ran while one was open for 0% of the time, Pallas kernels for 0%

profile of v1, /device:TPU:8, one launch (start us, length us, event | category | flops | bytes accessed | tf_op | source)
XLA Modules:
  0.0 84.7 jit_solution(6620812458002171069)
XLA Ops:
  0.0 2.0 %pad_maximum_fusion = bf16[32,32,256]{2,1,0:T(8,128)(2,1)} fusion(bf16[8,32,256]{2,1,0:T(8,128)(2,1)} %param.21), kind=kLoop, calls=%fused_computation | loop fusion | flops 786432 | bytes 655360 | tf_op jit(solution)/shard_map/concatenate | solution.py:157
  2.0 0.0 copy-start.3
  2.0 0.0 copy-start.4
  2.0 0.0 copy-start.5
  2.0 0.0 copy-start.6
  2.0 0.0 copy-start.7
  2.0 0.0 copy-start.12
  2.0 9.6 %all-to-all-start = ((bf16[32,32,256]{2,1,0:T(8,128)(2,1)}), bf16[32,32,256]{2,1,0:T(8,128)(2,1)S(1)}, u32[]{:S(2)}, u32[]{:S(2)}) async-start(bf16[32,32,256]{2,1,0:T(8,128)(2,1)} %pad_maximum_fusion), calls=%async_computation | async-start | bytes 1048576 | tf_op jit(solution)/shard_map/all_to_all | solution.py:156
  11.6 0.0 copy-start.16
  11.6 0.0 copy-start.17
  11.6 0.6 copy-done.16
  12.3 0.0 copy-done.17
  12.3 14.7 %all-to-all-done = bf16[32,32,256]{2,1,0:T(8,128)(2,1)S(1)} async-done(((bf16[32,32,256]{2,1,0:T(8,128)(2,1)}), bf16[32,32,256]{2,1,0:T(8,128)(2,1)S(1)}, u32[]{:S(2)}, u32[]{:S(2)}) %all-to-all-start) | async-done | bytes 524320 | tf_op jit(solution)/shard_map/all_to_all | solution.py:156
  27.0 0.0 copy-start.13
  27.0 0.0 copy-done.3
  27.0 0.0 copy-done.4
  27.0 0.0 copy-done.5
  27.0 0.0 copy-done.6
  27.0 0.0 copy-done.7
  27.1 0.0 copy-done.12
  27.1 0.6 copy-done.13
  27.7 0.0 copy-start.1
  27.7 0.0 copy-start.2
  27.7 0.0 copy-start.8
  27.7 0.0 copy-start.9
  27.7 0.0 copy-start.10
  27.7 0.0 copy-start.11
  27.7 7.9 %shard_map.199 = bf16[2,512,128]{2,1,0:T(8,128)(2,1)} custom-call(s32[1]{0:T(128)} %bitcast.1.yl_ref, f32[8]{0:T(128)S(1)} %get-tuple-element.6.ratio_ref, f32[8]{0:T(128)S(1)} %get-tuple-element.5.scale_ref, bf16[1024,256]{1,0:T(8,128)(2,1)S(1)} %bitcast.10, f32[1,256]{1,0:T(1,128)S(1)} %bitcast.14, bf16[256,256]{1,0:T(8,128)(2,1)S(1)} %copy-done.4, ...), custom_call_target="tpu_custom_call" | custom-call | tf_op jit(solution)/shard_map/pallas_call | solution.py:159
  35.6 0.0 copy-start
  35.6 0.0 copy-start.15
  35.6 14.4 %all-to-all-start.1 = ((bf16[128,8,128]{2,1,0:T(8,128)(2,1)}), bf16[128,8,128]{2,1,0:T(8,128)(2,1)S(1)}, u32[]{:S(2)}, u32[]{:S(2)}) async-start(bf16[128,8,128]{2,1,0:T(8,128)(2,1)} %bitcast.4), calls=%async_computation.1 | async-start | bytes 524288 | tf_op jit(solution)/shard_map/all_to_all | solution.py:176
  50.0 0.0 copy-start.18
  50.0 0.0 copy-start.19
  50.0 0.6 copy-done.18
  50.7 0.0 copy-done.19
  50.7 17.7 %all-to-all-done.1 = bf16[128,8,128]{2,1,0:T(8,128)(2,1)S(1)} async-done(((bf16[128,8,128]{2,1,0:T(8,128)(2,1)}), bf16[128,8,128]{2,1,0:T(8,128)(2,1)S(1)}, u32[]{:S(2)}, u32[]{:S(2)}) %all-to-all-start.1) | async-done | bytes 262176 | tf_op jit(solution)/shard_map/all_to_all | solution.py:176
  68.4 0.0 copy-done.1
  68.4 0.0 copy-done.2
  68.4 0.0 copy-done.8
  68.4 0.0 copy-done.9
  68.5 0.0 copy-done.10
  68.5 0.0 copy-done.11
  68.5 0.0 copy-done
  68.5 0.0 copy-done.15
  68.5 0.6 copy-done.14
  69.1 2.7 %shard_map.200 = bf16[8,4,8,256]{3,2,1,0:T(8,128)(2,1)S(1)} custom-call(s32[1]{0:T(128)} %bitcast.yh_ref, f32[8]{0:T(128)S(1)} %get-tuple-element.8.scale_ref, f32[8]{0:T(128)S(1)} %get-tuple-element.7.slope_ref, bf16[1024,128]{1,0:T(8,128)(2,1)S(1)} %bitcast.11, f32[1,256]{1,0:T(1,128)S(1)} %bitcast.15, bf16[256,256]{1,0:T(8,128)(2,1)S(1)} %copy-done.8, ...), custom_call_target="tpu_custom_call" | custom-call | tf_op jit(solution)/shard_map/pallas_call | solution.py:179
  71.9 12.0 %all_to_all.15 = bf16[8,32,256]{2,1,0:T(8,128)(2,1)S(1)} all-to-all(bf16[8,32,256]{2,1,0:T(8,128)(2,1)S(1)} %bitcast.12), channel_id=1, replica_groups=mesh['yl'=4,'x'=4,'c'=2,'z'=8,'yh'=2] {'z'}, dimensions={0} | all-to-all | bytes 262144 | tf_op jit(solution)/shard_map/all_to_all | solution.py:194
  83.8 0.8 shard_map.201
  (3 shorter events, 0.0 us)
Async XLA Ops:
  2.0 25.0 %copy-start.3 = (bf16[1024,128]{1,0:T(8,128)(2,1)S(1)}, bf16[1024,128]{1,0:T(8,128)(2,1)}, u32[]{:S(2)}) copy-start(bf16[1024,128]{1,0:T(8,128)(2,1)} %constant.22.clone.keyf_ref) | copy-start | bytes 786436
  2.0 25.0 %copy-start.4 = (bf16[256,256]{1,0:T(8,128)(2,1)S(1)}, bf16[256,256]{1,0:T(8,128)(2,1)}, u32[]{:S(2)}) copy-start(bf16[256,256]{1,0:T(8,128)(2,1)} %wq_ref.2) | copy-start | bytes 393220
  2.0 25.0 %copy-start.5 = (bf16[256,256]{1,0:T(8,128)(2,1)S(1)}, bf16[256,256]{1,0:T(8,128)(2,1)}, u32[]{:S(2)}) copy-start(bf16[256,256]{1,0:T(8,128)(2,1)} %wk_ref.2) | copy-start | bytes 393220
  2.0 25.0 %copy-start.6 = (bf16[256,256]{1,0:T(8,128)(2,1)S(1)}, bf16[256,256]{1,0:T(8,128)(2,1)}, u32[]{:S(2)}) copy-start(bf16[256,256]{1,0:T(8,128)(2,1)} %wv_ref.2) | copy-start | bytes 393220
  2.0 25.0 %copy-start.7 = (bf16[256,256]{1,0:T(8,128)(2,1)S(1)}, bf16[256,256]{1,0:T(8,128)(2,1)}, u32[]{:S(2)}) copy-start(bf16[256,256]{1,0:T(8,128)(2,1)} %wo_ref.2) | copy-start | bytes 393220
  2.0 25.0 %copy-start.12 = (f32[16,1024]{1,0:T(8,128)S(1)}, f32[16,1024]{1,0:T(8,128)}, u32[]{:S(2)}) copy-start(f32[16,1024]{1,0:T(8,128)} %constant.23.clone.wave_ref) | copy-start | bytes 196612
  2.0 25.0 %all-to-all-start = ((bf16[32,32,256]{2,1,0:T(8,128)(2,1)}), bf16[32,32,256]{2,1,0:T(8,128)(2,1)S(1)}, u32[]{:S(2)}, u32[]{:S(2)}) async-start(bf16[32,32,256]{2,1,0:T(8,128)(2,1)} %pad_maximum_fusion), calls=%async_computation | async-start | bytes 1048576 | tf_op jit(solution)/shard_map/all_to_all | solution.py:156
  11.6 0.7 copy-start.16
  11.6 0.7 copy-start.17
  27.0 0.7 copy-start.13
  27.7 40.7 %copy-start.1 = (bf16[256,1024]{1,0:T(8,128)(2,1)S(1)}, bf16[256,1024]{1,0:T(8,128)(2,1)}, u32[]{:S(2)}) copy-start(bf16[256,1024]{1,0:T(8,128)(2,1)} %wu_ref.1) | copy-start | bytes 1572868
  27.7 40.7 %copy-start.2 = (bf16[1024,256]{1,0:T(8,128)(2,1)S(1)}, bf16[1024,256]{1,0:T(8,128)(2,1)}, u32[]{:S(2)}) copy-start(bf16[1024,256]{1,0:T(8,128)(2,1)} %wd_ref.1) | copy-start | bytes 1572868
  27.7 40.7 %copy-start.8 = (bf16[256,256]{1,0:T(8,128)(2,1)S(1)}, bf16[256,256]{1,0:T(8,128)(2,1)}, u32[]{:S(2)}) copy-start(bf16[256,256]{1,0:T(8,128)(2,1)} %wq_ref.3) | copy-start | bytes 393220
  27.7 40.7 %copy-start.9 = (bf16[256,256]{1,0:T(8,128)(2,1)S(1)}, bf16[256,256]{1,0:T(8,128)(2,1)}, u32[]{:S(2)}) copy-start(bf16[256,256]{1,0:T(8,128)(2,1)} %wk_ref.3) | copy-start | bytes 393220
  27.7 40.7 %copy-start.10 = (bf16[256,256]{1,0:T(8,128)(2,1)S(1)}, bf16[256,256]{1,0:T(8,128)(2,1)}, u32[]{:S(2)}) copy-start(bf16[256,256]{1,0:T(8,128)(2,1)} %wv_ref.3) | copy-start | bytes 393220
  27.7 40.7 %copy-start.11 = (bf16[256,256]{1,0:T(8,128)(2,1)S(1)}, bf16[256,256]{1,0:T(8,128)(2,1)}, u32[]{:S(2)}) copy-start(bf16[256,256]{1,0:T(8,128)(2,1)} %wo_ref.3) | copy-start | bytes 393220
  35.6 32.8 %copy-start = (bf16[256,1024]{1,0:T(8,128)(2,1)S(1)}, bf16[256,1024]{1,0:T(8,128)(2,1)}, u32[]{:S(2)}) copy-start(bf16[256,1024]{1,0:T(8,128)(2,1)} %wg_ref.1) | copy-start | bytes 1572868
  35.6 32.8 %copy-start.15 = (f32[256]{0:T(256)S(1)}, f32[256]{0:T(256)}, u32[]{:S(2)}) copy-start(f32[256]{0:T(256)} %param.36) | copy-start | bytes 3076
  35.6 32.8 %all-to-all-start.1 = ((bf16[128,8,128]{2,1,0:T(8,128)(2,1)}), bf16[128,8,128]{2,1,0:T(8,128)(2,1)S(1)}, u32[]{:S(2)}, u32[]{:S(2)}) async-start(bf16[128,8,128]{2,1,0:T(8,128)(2,1)} %bitcast.4), calls=%async_computation.1 | async-start | bytes 524288 | tf_op jit(solution)/shard_map/all_to_all | solution.py:176
  50.0 0.7 copy-start.18
  50.0 0.7 copy-start.19
  68.4 0.7 copy-start.14

commit v2 on v1

--- a/solution.py
+++ b/solution.py
@@ -28,12 +28,28 @@
     return (values * factor * gain).astype(BF16)
 
 
+def prep_kernel(*refs):
+    x_ref, gains, heads, (dup_ref, table_ref) = refs[0], refs[1:4], refs[4:8], refs[8:]
+    for j in range(YL):
+        dup_ref[j] = x_ref[...]
+    for j, ref in enumerate(gains):
+        table_ref[j : j + 1, :] = ref[...]
+    temp_lon, bias_lon, temp_lat, bias_lat = heads
+    root = 1.0 / math.sqrt(HEAD)
+    for h in range(HEADS):
+        rows = [jnp.full((1, D), ref[h], F32) for ref in heads]
+        table_ref[8 + h : 9 + h, :] = rows[1] / (rows[0] * root)
+        table_ref[16 + h : 17 + h, :] = rows[0] * (root * LOG2E)
+        table_ref[24 + h : 25 + h, :] = rows[2] * (root * LOG2E)
+        table_ref[32 + h : 33 + h, :] = rows[3] * LOG2E
+
+
 def row_kernel(
-    yl_ref, ratio_ref, scale_ref, x_ref, gain_ref, wq_ref, wk_ref, wv_ref, wo_ref, keyf_ref, wave_ref,
+    x_ref, table_ref, wq_ref, wk_ref, wv_ref, wo_ref, keyf_ref, wave_ref,
     out_ref, norm_s, kext_s, att_s, first_s, send_s,
 ):
-    own = pl.ds(pl.multiple_of(yl_ref[0] * 256, 256), 256)
-    norm_s[...] = normed(x_ref[...].astype(F32), gain_ref[...])
+    own = pl.ds(pl.multiple_of(lax.axis_index("yl") * 256, 256), 256)
+    norm_s[...] = normed(x_ref[...].astype(F32), table_ref[0:1, :])
     keys = dot(norm_s[...], wk_ref[...]).astype(BF16)
     for g in range(2):
         kext_s[g, :, :128] = keys[:, 128 * g : 128 * g + 128]
@@ -43,9 +59,10 @@
     wave = wave_ref[:, own]
     low_rows = lax.broadcasted_iota(jnp.int32, wave.shape, 0) % 3 == 2
     ones = jnp.ones((16, 1024), BF16)
-    for h in range(HEADS):
+
+    def scored(h):
         at = HEAD * (h % 4)
-        full = wave * ratio_ref[h]
+        full = wave * table_ref[8 + h : 9 + h, :]
         high = full.astype(BF16).astype(F32)
         feats = jnp.where(low_rows, full - high, high).astype(BF16)
         parts = [qs_t[HEAD * h : HEAD * h + HEAD], feats, jnp.zeros((112, 256), BF16)]
@@ -53,11 +70,32 @@
             parts.insert(1, jnp.zeros((128 - at - HEAD, 256), BF16))
         if at:
             parts.insert(0, jnp.zeros((at, 256), BF16))
-        scores = dot(kext_s[h // 4], jnp.concatenate(parts, axis=0))
-        peak = jnp.max(scores, axis=0, keepdims=True)
-        expo = jnp.exp2((scores - peak) * scale_ref[h]).astype(BF16)
+        masked = jnp.concatenate(parts, axis=0)
+        scores, peak = [], None
+        for c in range(0, 1024, 512):
+            scores.append(dot(kext_s[h // 4, c : c + 512, :], masked))
+            for i in range(0, 512, 128):
+                some = scores[-1][i : i + 128]
+                peak = some if peak is None else jnp.maximum(peak, some)
+        for n in (64, 32, 16, 8):
+            peak = jnp.maximum(peak[:n], peak[n : 2 * n])
+        return scores, jnp.max(peak, axis=0, keepdims=True)
+
+    def mix(h, expo):
         mixed = dot(jnp.concatenate([vals_t[HEAD * h : HEAD * h + HEAD], ones], axis=0), expo)
         att_s[HEAD * h : HEAD * h + HEAD, :] = mixed[:HEAD] / mixed[HEAD : HEAD + 1]
+
+    ahead, behind = scored(0), None
+    for h in range(HEADS):
+        scores, peak = ahead
+        if h + 1 < HEADS:
+            ahead = scored(h + 1)
+        scale = table_ref[16 + h : 17 + h, :]
+        expo = jnp.concatenate([jnp.exp2((s - peak) * scale).astype(BF16) for s in scores], axis=0)
+        if behind is not None:
+            mix(h - 1, behind)
+        behind = expo
+    mix(HEADS - 1, behind)
     attended = att_s[...].T.astype(BF16)
     first_s[...] = x_ref[own, :].astype(F32) + dot(attended, wo_ref[...])
     for xc in range(8):
@@ -71,7 +109,7 @@
 
 
 def col_kernel(
-    yh_ref, scale_ref, slope_ref, x_ref, gain_ref, wq_ref, wk_ref, wv_ref, wo_ref, gain2_ref, wg_ref, wu_ref, wd_ref,
+    x_ref, table_ref, wq_ref, wk_ref, wv_ref, wo_ref, wg_ref, wu_ref, wd_ref,
     out_ref, wide_s, first_s, norm_s,
 ):
     wide_s[...] = x_ref[...].astype(F32)
@@ -79,8 +117,9 @@
         for f in range(2):
             first_s[k, :, 128 * f : 128 * f + 128] = wide_s[pl.ds(4 * f + k, 128, stride=8), :]
     for k in range(4):
-        norm_s[k] = normed(first_s[k], gain_ref[...])
-    own = pl.ds(pl.multiple_of(yh_ref[0] * 64, 64), 64)
+        norm_s[k] = normed(first_s[k], table_ref[1:2, :])
+    yh = lax.axis_index("yh")
+    own = pl.ds(pl.multiple_of(yh * 64, 64), 64)
     flat = norm_s[...].reshape(512, D)
     keys = dot(flat, wk_ref[...]).astype(BF16)
     vals = dot(flat, wv_ref[...]).astype(BF16)
@@ -88,7 +127,7 @@
     qs = dot(mine, wq_ref[...])
     a = lax.broadcasted_iota(jnp.int32, (64, 128), 0)
     b = lax.broadcasted_iota(jnp.int32, (64, 128), 1)
-    lat_a = 16 * (a // 8) + 8 * yh_ref[0] + a % 8
+    lat_a = 16 * (a // 8) + 8 * yh + a % 8
     lat_b = 16 * ((b // 8) % 8) + 8 * (b // 64) + b % 8
     spread = jnp.abs(lat_a - lat_b).astype(F32) * (1.0 / 128)
     head_of = lax.broadcasted_iota(jnp.int32, (64, D), 1) // HEAD
@@ -100,7 +139,10 @@
             masked, keys[128 * k : 128 * k + 128], (((1,), (1,)), ((), ())), preferred_element_type=F32
         )
         scores = jnp.concatenate(
-            [raw[64 * h : 64 * h + 64] * scale_ref[h] + spread * slope_ref[h] for h in range(HEADS)], axis=0
+            [
+                raw[64 * h : 64 * h + 64] * table_ref[24 + h : 25 + h, :128] + spread * table_ref[32 + h : 33 + h, :128]
+                for h in range(HEADS)
+            ], axis=0
         )
         expo = jnp.exp2(scores - jnp.max(scores, axis=-1, keepdims=True))
         denom = jnp.sum(expo, axis=-1, keepdims=True)
@@ -111,7 +153,7 @@
         mixes.append(total.astype(BF16))
     resid = jnp.concatenate([first_s[k, own, :] for k in range(4)], axis=0)
     second = resid + dot(jnp.concatenate(mixes, axis=0), wo_ref[...])
-    third = normed(second, gain2_ref[...])
+    third = normed(second, table_ref[2:3, :])
     gate = dot(third, wg_ref[...])
     upper = dot(third, wu_ref[...])
     hidden = (gate / (1.0 + jnp.exp(-gate)) * upper).astype(BF16)
@@ -149,17 +191,21 @@
     norm_lat, query_lat, key_lat, value_lat, out_lat, temp_lat, bias_lat, norm_mlp, w_gate, w_up, w_down,
 ):
     keyf, wave = tables()
-    yl = lax.axis_index("yl").astype(jnp.int32).reshape(1)
-    yh = lax.axis_index("yh").astype(jnp.int32).reshape(1)
-    scale_lon = temp_lon / math.sqrt(HEAD)
-    scale_lat = temp_lat * (LOG2E / math.sqrt(HEAD))
-    row = lax.all_to_all(
-        jnp.concatenate([fields] * YL, axis=0), ("yl", "x", "c"), split_axis=0, concat_axis=0, tiled=True
-    )
+    four, table = pl.pallas_call(
+        prep_kernel,
+        out_shape=(jax.ShapeDtypeStruct((YL, 8, 32, D), BF16), jax.ShapeDtypeStruct((40, D), F32)),
+        in_specs=[VMEM] * 4 + [SMEM] * 4,
+        out_specs=(VMEM, VMEM),
+        compiler_params=PARAMS,
+    )(
+        fields, norm_lon.reshape(1, D), norm_lat.reshape(1, D), norm_mlp.reshape(1, D),
+        temp_lon, bias_lon, temp_lat, bias_lat,
+    )
+    row = lax.all_to_all(four.reshape(32, 32, D), ("yl", "x", "c"), split_axis=0, concat_axis=0, tiled=True)
     sent = pl.pallas_call(
         row_kernel,
         out_shape=jax.ShapeDtypeStruct((2, 512, 128), BF16),
-        in_specs=[SMEM] * 3 + [VMEM] * 8,
+        in_specs=[VMEM] * 8,
         out_specs=VMEM,
         scratch_shapes=[
             pltpu.VMEM((1024, D), BF16),
@@ -170,8 +216,7 @@
         ],
         compiler_params=PARAMS,
     )(
-        yl, bias_lon / scale_lon, scale_lon * LOG2E, row.reshape(1024, D), norm_lon.reshape(1, D),
-        query_lon, key_lon, value_lon, out_lon, keyf, wave,
+        row.reshape(1024, D), table, query_lon, key_lon, value_lon, out_lon, keyf, wave,
     )
     cols = lax.all_to_all(
         sent.reshape(128, 8, 128), ("yh", "z", "x", "c"), split_axis=0, concat_axis=0, tiled=True
@@ -179,7 +224,7 @@
     done = pl.pallas_call(
         col_kernel,
         out_shape=jax.ShapeDtypeStruct((8, 4, 8, D), BF16),
-        in_specs=[SMEM] * 3 + [VMEM] * 10,
+        in_specs=[VMEM] * 9,
         out_specs=VMEM,
         scratch_shapes=[
             pltpu.VMEM((1024, 128), F32),
@@ -188,8 +233,7 @@
         ],
         compiler_params=PARAMS,
     )(
-        yh, scale_lat, bias_lat * LOG2E, cols.reshape(1024, 128), norm_lat.reshape(1, D),
-        query_lat, key_lat, value_lat, out_lat, norm_mlp.reshape(1, D), w_gate, w_up, w_down,
+        cols.reshape(1024, 128), table, query_lat, key_lat, value_lat, out_lat, w_gate, w_up, w_down,
     )
     home = lax.all_to_all(done.reshape(8, 32, D), "z", split_axis=0, concat_axis=0, tiled=True)
     return pl.pallas_call(

time: 85.1 us -> 79.1 us (0.929)
  blocking collectives: 12 us -> 69.3 us
  waiting for transfers between devices: 32.5 us -> 0 us
  starting transfers between devices: 23.9 us -> 0 us
  Pallas kernels: 11.5 us -> 7.58 us
  other arithmetic: 2.01 us -> 0 us
  local copies, waits for them, and re-layouts: 2.63 us -> 1.71 us
    all_to_all x0 -> x2, blocking collectives: none -> 57.3 us  [the longest x1 33.3 us: body(): lax.all_to_all(sent.reshape(128, 8, 128), ('yh', 'z', 'x', 'c'), split_ax...]
    all_to_all x2 -> x0, waiting for transfers between devices: 32.5 us -> none  [the longest x1 17.7 us: body(): lax.all_to_all(sent.reshape(128, 8, 128), ('yh', 'z', 'x', 'c'), split_ax...]
    all_to_all x2 -> x0, starting transfers between devices: 23.9 us -> none  [the longest x1 14.4 us: body(): lax.all_to_all(sent.reshape(128, 8, 128), ('yh', 'z', 'x', 'c'), split_ax...]
    pallas_call x1, Pallas kernels: 7.91 us -> 3.91 us  [body(): pl.pallas_call(row_kernel, out_shape=jax.ShapeDtypeStruct((2, 512, 128),...]
    concatenate x1 -> x0, other arithmetic: 2 us -> none  [body(): jnp.concatenate([fields] * YL, axis=0)]
    unnamed x40 -> x42, local copies, waits for them, and re-layouts: 2.63 us -> 1.71 us
  transfers between devices with their start and end apart: 2 -> 0, of which waited for: 2 -> 0; matrix products, arithmetic and copies ran while one was open for 0% -> 0% of each run, Pallas kernels for 0% -> 0%
where the time goes in v2:
time: 79.1 us; the launch traced here: 78.8 us
  blocking collectives  69.3 us (88%)
  Pallas kernels  7.58 us (10%)
  local copies, waits for them, and re-layouts  1.71 us (2%)
    all_to_all x1, blocking collectives, body(): lax.all_to_all(sent.reshape(128, 8, 128), ('yh', 'z', 'x', 'c'), split_ax...  33.3 us
    all_to_all x1, blocking collectives, body(): lax.all_to_all(four.reshape(32, 32, D), ('yl', 'x', 'c'), split_axis=0, c...  24.1 us
    all_to_all x1, blocking collectives, body(): lax.all_to_all(done.reshape(8, 32, D), 'z', split_axis=0, concat_axis=0,...  12 us
    pallas_call x1, Pallas kernels, body(): pl.pallas_call(row_kernel, out_shape=jax.ShapeDtypeStruct((2, 512, 128),...  3.91 us
    pallas_call x1, Pallas kernels, body(): pl.pallas_call(col_kernel, out_shape=jax.ShapeDtypeStruct((8, 4, 8, D), B...  2.25 us
    unnamed x42, local copies, waits for them, and re-layouts  1.71 us

profile of v2, /device:TPU:8, one launch (start us, length us, event | category | flops | bytes accessed | tf_op | source)
XLA Modules:
  0.0 78.8 jit_solution(11832674423606746703)
XLA Ops:
  0.0 0.0 copy-start.18
  0.0 0.0 copy-start.19
  0.0 0.0 copy-start.20
  0.0 0.0 copy-start.15
  0.0 0.0 copy-start.16
  0.0 0.0 copy-start.14
  0.0 0.0 copy-start.17
  0.0 0.6 copy-done.18
  0.7 0.0 copy-done.19
  0.7 0.0 copy-done.20
  0.7 0.0 copy-done.15
  0.7 0.0 copy-done.16
  0.7 0.0 copy-done.14
  0.8 0.0 copy-done.17
  0.8 0.9 %copy-done.12 = bf16[8,32,256]{2,1,0:T(8,128)(2,1)S(1)} copy-done((bf16[8,32,256]{2,1,0:T(8,128)(2,1)S(1)}, bf16[8,32,256]{2,1,0:T(8,128)(2,1)}, u32[]{:S(2)}) %copy-start.12) | copy-done | bytes 131096
  1.7 0.6 shard_map.199
  2.3 0.0 copy-start.3
  2.3 0.0 copy-start.4
  2.3 0.0 copy-start.5
  2.3 0.0 copy-start.6
  2.3 0.0 copy-start.7
  2.3 0.0 copy-start.13
  2.4 24.1 %all_to_all.15 = bf16[32,32,256]{2,1,0:T(8,128)(2,1)S(1)} all-to-all(bf16[32,32,256]{2,1,0:T(8,128)(2,1)S(1)} %bitcast.13), channel_id=1, replica_groups=mesh['yl'=4,'x'=4,'c'=2,'z'=8,'yh'=2] {'yl','x','c'}, dimensions={0} | all-to-all | bytes 1048576 | tf_op jit(solution)/shard_map/all_to_all | solution.py:204
  26.4 0.0 copy-done.3
  26.4 0.0 copy-done.4
  26.4 0.0 copy-done.5
  26.4 0.0 copy-done.6
  26.4 0.0 copy-done.7
  26.4 0.0 copy-done.13
  26.5 0.0 copy-start.1
  26.5 0.0 copy-start.2
  26.5 0.0 copy-start.8
  26.5 0.0 copy-start.9
  26.5 0.0 copy-start.10
  26.5 0.0 copy-start.11
  26.5 3.9 %shard_map.200 = bf16[2,512,128]{2,1,0:T(8,128)(2,1)S(1)} custom-call(bf16[1024,256]{1,0:T(8,128)(2,1)S(1)} %bitcast.9, f32[40,256]{1,0:T(8,128)S(1)} %get-tuple-element.8.table_ref, bf16[256,256]{1,0:T(8,128)(2,1)S(1)} %copy-done.4, bf16[256,256]{1,0:T(8,128)(2,1)S(1)} %copy-done.5, bf16[256,256]{1,0:T(8,128)(2,1)S(1)} %copy-done.6, ...), custom_call_target="tpu_custom_call" | custom-call | tf_op jit(solution)/shard_map/pallas_call | solution.py:205
  30.4 0.0 copy-start
  30.5 33.3 %all_to_all.16 = bf16[128,8,128]{2,1,0:T(8,128)(2,1)S(1)} all-to-all(bf16[128,8,128]{2,1,0:T(8,128)(2,1)S(1)} %bitcast.10), channel_id=1, replica_groups=mesh['yl'=4,'x'=4,'c'=2,'z'=8,'yh'=2] {'yh','z','x','c'}, dimensions={0} | all-to-all | bytes 524288 | tf_op jit(solution)/shard_map/all_to_all | solution.py:221
  63.7 0.0 copy-done.1
  63.7 0.0 copy-done.2
  63.7 0.0 copy-done.8
  63.7 0.0 copy-done.9
  63.7 0.0 copy-done.10
  63.8 0.0 copy-done.11
  63.8 0.0 copy-done
  63.8 2.2 %shard_map.201 = bf16[8,4,8,256]{3,2,1,0:T(8,128)(2,1)S(1)} custom-call(bf16[1024,128]{1,0:T(8,128)(2,1)S(1)} %bitcast.11, f32[40,256]{1,0:T(8,128)S(1)} %get-tuple-element.8.table_ref, bf16[256,256]{1,0:T(8,128)(2,1)S(1)} %copy-done.8, bf16[256,256]{1,0:T(8,128)(2,1)S(1)} %copy-done.9, bf16[256,256]{1,0:T(8,128)(2,1)S(1)} %copy-done.10, ...), custom_call_target="tpu_custom_call" | custom-call | tf_op jit(solution)/shard_map/pallas_call | solution.py:224
  66.0 12.0 %all_to_all.17 = bf16[8,32,256]{2,1,0:T(8,128)(2,1)S(1)} all-to-all(bf16[8,32,256]{2,1,0:T(8,128)(2,1)S(1)} %bitcast.12), channel_id=1, replica_groups=mesh['yl'=4,'x'=4,'c'=2,'z'=8,'yh'=2] {'z'}, dimensions={0} | all-to-all | bytes 262144 | tf_op jit(solution)/shard_map/all_to_all | solution.py:238
  78.0 0.8 %shard_map.202 = bf16[8,32,256]{2,1,0:T(8,128)(2,1)} custom-call(bf16[256,256]{1,0:T(8,128)(2,1)S(1)} %bitcast.14), custom_call_target="tpu_custom_call" | custom-call | tf_op jit(solution)/shard_map/pallas_call | solution.py:239
  (1 shorter events, 0.0 us)
Async XLA Ops:
  0.0 0.7 copy-start.18
  0.0 0.7 copy-start.19
  0.0 0.7 copy-start.20
  0.0 0.7 copy-start.15
  0.0 0.7 copy-start.16
  0.0 0.7 copy-start.14
  0.0 0.7 copy-start.17
  0.8 0.9 %copy-start.12 = (bf16[8,32,256]{2,1,0:T(8,128)(2,1)S(1)}, bf16[8,32,256]{2,1,0:T(8,128)(2,1)}, u32[]{:S(2)}) copy-start(bf16[8,32,256]{2,1,0:T(8,128)(2,1)} %refs_0_.1) | copy-start | bytes 393220
  2.3 24.1 %copy-start.3 = (bf16[1024,128]{1,0:T(8,128)(2,1)S(1)}, bf16[1024,128]{1,0:T(8,128)(2,1)}, u32[]{:S(2)}) copy-start(bf16[1024,128]{1,0:T(8,128)(2,1)} %constant.4.clone.keyf_ref) | copy-start | bytes 786436
  2.3 24.1 %copy-start.4 = (bf16[256,256]{1,0:T(8,128)(2,1)S(1)}, bf16[256,256]{1,0:T(8,128)(2,1)}, u32[]{:S(2)}) copy-start(bf16[256,256]{1,0:T(8,128)(2,1)} %wq_ref.2) | copy-start | bytes 393220
  2.3 24.1 %copy-start.5 = (bf16[256,256]{1,0:T(8,128)(2,1)S(1)}, bf16[256,256]{1,0:T(8,128)(2,1)}, u32[]{:S(2)}) copy-start(bf16[256,256]{1,0:T(8,128)(2,1)} %wk_ref.2) | copy-start | bytes 393220
  2.3 24.1 %copy-start.6 = (bf16[256,256]{1,0:T(8,128)(2,1)S(1)}, bf16[256,256]{1,0:T(8,128)(2,1)}, u32[]{:S(2)}) copy-start(bf16[256,256]{1,0:T(8,128)(2,1)} %wv_ref.2) | copy-start | bytes 393220
  2.3 24.1 %copy-start.7 = (bf16[256,256]{1,0:T(8,128)(2,1)S(1)}, bf16[256,256]{1,0:T(8,128)(2,1)}, u32[]{:S(2)}) copy-start(bf16[256,256]{1,0:T(8,128)(2,1)} %wo_ref.2) | copy-start | bytes 393220
  2.3 24.1 %copy-start.13 = (f32[16,1024]{1,0:T(8,128)S(1)}, f32[16,1024]{1,0:T(8,128)}, u32[]{:S(2)}) copy-start(f32[16,1024]{1,0:T(8,128)} %constant.5.clone.wave_ref) | copy-start | bytes 196612
  26.5 37.3 %copy-start.1 = (bf16[256,1024]{1,0:T(8,128)(2,1)S(1)}, bf16[256,1024]{1,0:T(8,128)(2,1)}, u32[]{:S(2)}) copy-start(bf16[256,1024]{1,0:T(8,128)(2,1)} %wu_ref.1) | copy-start | bytes 1572868
  26.5 37.3 %copy-start.2 = (bf16[1024,256]{1,0:T(8,128)(2,1)S(1)}, bf16[1024,256]{1,0:T(8,128)(2,1)}, u32[]{:S(2)}) copy-start(bf16[1024,256]{1,0:T(8,128)(2,1)} %wd_ref.1) | copy-start | bytes 1572868
  26.5 37.3 %copy-start.8 = (bf16[256,256]{1,0:T(8,128)(2,1)S(1)}, bf16[256,256]{1,0:T(8,128)(2,1)}, u32[]{:S(2)}) copy-start(bf16[256,256]{1,0:T(8,128)(2,1)} %wq_ref.3) | copy-start | bytes 393220
  26.5 37.3 %copy-start.9 = (bf16[256,256]{1,0:T(8,128)(2,1)S(1)}, bf16[256,256]{1,0:T(8,128)(2,1)}, u32[]{:S(2)}) copy-start(bf16[256,256]{1,0:T(8,128)(2,1)} %wk_ref.3) | copy-start | bytes 393220
  26.5 37.2 %copy-start.10 = (bf16[256,256]{1,0:T(8,128)(2,1)S(1)}, bf16[256,256]{1,0:T(8,128)(2,1)}, u32[]{:S(2)}) copy-start(bf16[256,256]{1,0:T(8,128)(2,1)} %wv_ref.3) | copy-start | bytes 393220
  26.5 37.2 %copy-start.11 = (bf16[256,256]{1,0:T(8,128)(2,1)S(1)}, bf16[256,256]{1,0:T(8,128)(2,1)}, u32[]{:S(2)}) copy-start(bf16[256,256]{1,0:T(8,128)(2,1)} %wo_ref.3) | copy-start | bytes 393220
  30.4 33.3 %copy-start = (bf16[256,1024]{1,0:T(8,128)(2,1)S(1)}, bf16[256,1024]{1,0:T(8,128)(2,1)}, u32[]{:S(2)}) copy-start(bf16[256,1024]{1,0:T(8,128)(2,1)} %wg_ref.1) | copy-start | bytes 1572868

commit v3 on v2

--- a/solution.py
+++ b/solution.py
@@ -10,7 +10,7 @@
 from jax.sharding import Mesh
 from jax.sharding import PartitionSpec as P
 
-YL, X, C, Z, YH = 4, 4, 2, 8, 2
+YA, YB, X, C, Z, YH = 2, 2, 4, 2, 8, 2
 HEADS, HEAD, D = 8, 32, 256
 F32, BF16 = jnp.float32, jnp.bfloat16
 LOG2E = 1.0 / math.log(2.0)
@@ -28,13 +28,15 @@
     return (values * factor * gain).astype(BF16)
 
 
-def prep_kernel(*refs):
-    x_ref, gains, heads, (dup_ref, table_ref) = refs[0], refs[1:4], refs[4:8], refs[8:]
-    for j in range(YL):
-        dup_ref[j] = x_ref[...]
+def twice_kernel(x_ref, out_ref):
+    for j in range(YA):
+        out_ref[j] = x_ref[...]
+
+
+def table_kernel(*refs):
+    gains, heads, table_ref = refs[:3], refs[3:7], refs[7]
     for j, ref in enumerate(gains):
         table_ref[j : j + 1, :] = ref[...]
-    temp_lon, bias_lon, temp_lat, bias_lat = heads
     root = 1.0 / math.sqrt(HEAD)
     for h in range(HEADS):
         rows = [jnp.full((1, D), ref[h], F32) for ref in heads]
@@ -48,7 +50,8 @@
     x_ref, table_ref, wq_ref, wk_ref, wv_ref, wo_ref, keyf_ref, wave_ref,
     out_ref, norm_s, kext_s, att_s, first_s, send_s,
 ):
-    own = pl.ds(pl.multiple_of(lax.axis_index("yl") * 256, 256), 256)
+    place = 2 * lax.axis_index("c") + lax.axis_index("ya")
+    own = pl.ds(pl.multiple_of(place * 256, 256), 256)
     norm_s[...] = normed(x_ref[...].astype(F32), table_ref[0:1, :])
     keys = dot(norm_s[...], wk_ref[...]).astype(BF16)
     for g in range(2):
@@ -98,11 +101,11 @@
     mix(HEADS - 1, behind)
     attended = att_s[...].T.astype(BF16)
     first_s[...] = x_ref[own, :].astype(F32) + dot(attended, wo_ref[...])
-    for xc in range(8):
+    for part in range(8):
         for k in range(4):
-            rows = first_s[32 * xc + 8 * k : 32 * xc + 8 * k + 8, :]
-            send_s[pl.ds(8 * xc + k, 8, stride=64), :] = rows[:, :128]
-            send_s[pl.ds(8 * xc + 4 + k, 8, stride=64), :] = rows[:, 128:]
+            rows = first_s[32 * part + 8 * k : 32 * part + 8 * k + 8, :]
+            send_s[pl.ds(8 * part + k, 8, stride=64), :] = rows[:, :128]
+            send_s[pl.ds(8 * part + 4 + k, 8, stride=64), :] = rows[:, 128:]
     sent = send_s[...].astype(BF16)
     out_ref[0] = sent
     out_ref[1] = sent
@@ -175,7 +178,8 @@
 
 
 def tables():
-    angle = np.arange(1024) * (2.0 * math.pi / 1024)
+    order = np.arange(1024).reshape(YA * YB * X, C, 32).transpose(1, 0, 2).reshape(1024)
+    angle = order * (2.0 * math.pi / 1024)
     cos, sin = np.cos(angle), np.sin(angle)
     wave = np.zeros((16, 1024), np.float32)
     wave[0:3], wave[3:6] = cos, sin
@@ -191,17 +195,26 @@
     norm_lat, query_lat, key_lat, value_lat, out_lat, temp_lat, bias_lat, norm_mlp, w_gate, w_up, w_down,
 ):
     keyf, wave = tables()
-    four, table = pl.pallas_call(
-        prep_kernel,
-        out_shape=(jax.ShapeDtypeStruct((YL, 8, 32, D), BF16), jax.ShapeDtypeStruct((40, D), F32)),
-        in_specs=[VMEM] * 4 + [SMEM] * 4,
-        out_specs=(VMEM, VMEM),
+    twice = pl.pallas_call(
+        twice_kernel,
+        out_shape=jax.ShapeDtypeStruct((YA, 8, 32, D), BF16),
+        in_specs=[VMEM],
+        out_specs=VMEM,
+        compiler_params=PARAMS,
+    )(fields)
+    table = pl.pallas_call(
+        table_kernel,
+        out_shape=jax.ShapeDtypeStruct((40, D), F32),
+        in_specs=[VMEM] * 3 + [SMEM] * 4,
+        out_specs=VMEM,
         compiler_params=PARAMS,
     )(
-        fields, norm_lon.reshape(1, D), norm_lat.reshape(1, D), norm_mlp.reshape(1, D),
+        norm_lon.reshape(1, D), norm_lat.reshape(1, D), norm_mlp.reshape(1, D),
         temp_lon, bias_lon, temp_lat, bias_lat,
     )
-    row = lax.all_to_all(four.reshape(32, 32, D), ("yl", "x", "c"), split_axis=0, concat_axis=0, tiled=True)
+    twice, table = lax.optimization_barrier((twice, table))
+    half = lax.all_to_all(twice.reshape(16, 32, D), ("ya", "yb", "x"), split_axis=0, concat_axis=0, tiled=True)
+    row = lax.all_gather(half, "c", axis=0, tiled=True)
     sent = pl.pallas_call(
         row_kernel,
         out_shape=jax.ShapeDtypeStruct((2, 512, 128), BF16),
@@ -219,7 +232,7 @@
         row.reshape(1024, D), table, query_lon, key_lon, value_lon, out_lon, keyf, wave,
     )
     cols = lax.all_to_all(
-        sent.reshape(128, 8, 128), ("yh", "z", "x", "c"), split_axis=0, concat_axis=0, tiled=True
+        sent.reshape(128, 8, 128), ("yh", "z", "yb", "x"), split_axis=0, concat_axis=0, tiled=True
     )
     done = pl.pallas_call(
         col_kernel,
@@ -247,6 +260,6 @@
 
 
 def solution(mesh):
-    fine = Mesh(mesh.devices.reshape(YL, X, C, Z, YH), ("yl", "x", "c", "z", "yh"))
-    cells = P(("z", "yh"), ("yl", "x", "c"), None)
+    fine = Mesh(mesh.devices.reshape(YA, YB, X, C, Z, YH), ("ya", "yb", "x", "c", "z", "yh"))
+    cells = P(("z", "yh"), ("ya", "yb", "x", "c"), None)
     return jax.shard_map(body, mesh=fine, in_specs=(cells,) + (P(),) * 18, out_specs=cells, check_vma=False)

time: 79.1 us -> 74.2 us (0.938)
  blocking collectives: 69.3 us -> 64.5 us
    all_to_all x2, blocking collectives: 57.3 us -> 50.7 us  [the longest x1 33.6 us: body(): lax.all_to_all(sent.reshape(128, 8, 128), ('yh', 'z', 'yb', 'x'), split_a...]
    all_gather x0 -> x1, blocking collectives: none -> 2.31 us  [body(): row = lax.all_gather(half, 'c', axis=0, tiled=True)]
where the time goes in v3:
time: 74.2 us; the launch traced here: 74 us
  blocking collectives  64.5 us (87%)
  Pallas kernels  7.58 us (10%)
  local copies, waits for them, and re-layouts  1.68 us (2%)
    all_to_all x1, blocking collectives, body(): lax.all_to_all(sent.reshape(128, 8, 128), ('yh', 'z', 'yb', 'x'), split_a...  33.6 us
    all_to_all x1, blocking collectives, body(): lax.all_to_all(twice.reshape(16, 32, D), ('ya', 'yb', 'x'), split_axis=0,...  17.1 us
    all_to_all x1, blocking collectives, body(): lax.all_to_all(done.reshape(8, 32, D), 'z', split_axis=0, concat_axis=0,...  11.5 us
    pallas_call x1, Pallas kernels, body(): pl.pallas_call(row_kernel, out_shape=jax.ShapeDtypeStruct((2, 512, 128),...  3.91 us
    all_gather x1, blocking collectives, body(): row = lax.all_gather(half, 'c', axis=0, tiled=True)  2.31 us
    pallas_call x1, Pallas kernels, body(): pl.pallas_call(col_kernel, out_shape=jax.ShapeDtypeStruct((8, 4, 8, D), B...  2.25 us
    unnamed x42, local copies, waits for them, and re-layouts  1.68 us

profile of v3, /device:TPU:8, one launch (start us, length us, event | category | flops | bytes accessed | tf_op | source)
XLA Modules:
  0.0 74.0 jit_solution(18046053236390383167)
XLA Ops:
  0.0 0.0 copy-start.4
  0.0 0.9 %copy-done.4 = bf16[8,32,256]{2,1,0:T(8,128)(2,1)S(1)} copy-done((bf16[8,32,256]{2,1,0:T(8,128)(2,1)S(1)}, bf16[8,32,256]{2,1,0:T(8,128)(2,1)}, u32[]{:S(2)}) %copy-start.4) | copy-done | bytes 131096
  0.9 0.0 copy-start.15
  0.9 0.0 copy-start.16
  0.9 0.0 copy-start.18
  0.9 0.0 copy-start.19
  0.9 0.0 copy-start.20
  1.0 0.0 copy-start.14
  1.0 0.0 copy-start.17
  1.0 0.6 copy-done.15
  1.6 0.0 copy-done.16
  1.6 0.0 copy-done.18
  1.6 0.0 copy-done.19
  1.6 0.0 copy-done.20
  1.6 0.0 copy-done.14
  1.7 0.0 copy-done.17
  1.7 0.6 shard_map.200.table_ref
  2.3 0.0 copy-start.13
  2.3 17.1 %all_to_all.15 = bf16[16,32,256]{2,1,0:T(8,128)(2,1)S(1)} all-to-all(bf16[16,32,256]{2,1,0:T(8,128)(2,1)S(1)} %bitcast.12), channel_id=1, replica_groups=mesh['ya'=2,'yb'=2,'x'=4,'c'=2,'z'=8,'yh'=2] {'ya','yb','x'}, dimensions={0} | all-to-all | bytes 524288 | tf_op jit(solution)/shard_map/all_to_all | solution.py:216
  19.3 0.0 copy-start.3
  19.3 0.0 copy-start.5
  19.4 0.0 copy-start.8
  19.4 2.3 %all_gather.3 = bf16[32,32,256]{2,1,0:T(8,128)(2,1)S(1)} all-gather(bf16[16,32,256]{2,1,0:T(8,128)(2,1)S(1)} %all_to_all.15), channel_id=1, replica_groups=mesh['ya'=2,'yb'=2,'x'=4,'c'=2,'z'=8,'yh'=2] {'c'}, dimensions={0}, use_global_device_ids=true | all-gather | bytes 786432 | tf_op jit(solution)/shard_map/all_gather | solution.py:217
  21.7 0.0 copy-done.13
  21.7 0.0 copy-done.3
  21.7 0.0 copy-done.5
  21.7 0.0 copy-done.6
  21.7 0.0 copy-done.7
  21.7 0.0 copy-done.8
  21.7 0.0 copy-start.1
  21.7 0.0 copy-start.2
  21.7 0.0 copy-start.9
  21.8 0.0 copy-start.10
  21.8 0.0 copy-start.11
  21.8 0.0 copy-start.12
  21.8 3.9 %shard_map.201 = bf16[2,512,128]{2,1,0:T(8,128)(2,1)S(1)} custom-call(bf16[1024,256]{1,0:T(8,128)(2,1)S(1)} %bitcast.9, f32[40,256]{1,0:T(8,128)S(1)} %shard_map.200.table_ref, bf16[256,256]{1,0:T(8,128)(2,1)S(1)} %copy-done.5, bf16[256,256]{1,0:T(8,128)(2,1)S(1)} %copy-done.6, bf16[256,256]{1,0:T(8,128)(2,1)S(1)} %copy-done.7, ...), custom_call_target="tpu_custom_call" | custom-call | tf_op jit(solution)/shard_map/pallas_call | solution.py:218
  25.7 0.0 copy-start
  25.7 33.6 %all_to_all.16 = bf16[128,8,128]{2,1,0:T(8,128)(2,1)S(1)} all-to-all(bf16[128,8,128]{2,1,0:T(8,128)(2,1)S(1)} %bitcast.10), channel_id=1, replica_groups=mesh['ya'=2,'yb'=2,'x'=4,'c'=2,'z'=8,'yh'=2] {'yh','z','yb','x'}, dimensions={0} | all-to-all | bytes 524288 | tf_op jit(solution)/shard_map/all_to_all | solution.py:234
  59.4 0.0 copy-done.1
  59.4 0.0 copy-done.2
  59.4 0.0 copy-done.9
  59.4 0.0 copy-done.10
  59.4 0.0 copy-done.11
  59.4 0.0 copy-done.12
  59.4 0.0 copy-done
  59.4 2.2 %shard_map.202 = bf16[8,4,8,256]{3,2,1,0:T(8,128)(2,1)S(1)} custom-call(bf16[1024,128]{1,0:T(8,128)(2,1)S(1)} %bitcast.11, f32[40,256]{1,0:T(8,128)S(1)} %shard_map.200.table_ref, bf16[256,256]{1,0:T(8,128)(2,1)S(1)} %copy-done.9, bf16[256,256]{1,0:T(8,128)(2,1)S(1)} %copy-done.10, bf16[256,256]{1,0:T(8,128)(2,1)S(1)} %copy-done.11, ...), custom_call_target="tpu_custom_call" | custom-call | tf_op jit(solution)/shard_map/pallas_call | solution.py:237
  61.7 11.5 %all_to_all.17 = bf16[8,32,256]{2,1,0:T(8,128)(2,1)S(1)} all-to-all(bf16[8,32,256]{2,1,0:T(8,128)(2,1)S(1)} %bitcast.13), channel_id=1, replica_groups=mesh['ya'=2,'yb'=2,'x'=4,'c'=2,'z'=8,'yh'=2] {'z'}, dimensions={0} | all-to-all | bytes 262144 | tf_op jit(solution)/shard_map/all_to_all | solution.py:251
  73.1 0.8 %shard_map.203 = bf16[8,32,256]{2,1,0:T(8,128)(2,1)} custom-call(bf16[256,256]{1,0:T(8,128)(2,1)S(1)} %bitcast.14), custom_call_target="tpu_custom_call" | custom-call | tf_op jit(solution)/shard_map/pallas_call | solution.py:252
  (3 shorter events, 0.0 us)
Async XLA Ops:
  0.0 0.9 %copy-start.4 = (bf16[8,32,256]{2,1,0:T(8,128)(2,1)S(1)}, bf16[8,32,256]{2,1,0:T(8,128)(2,1)}, u32[]{:S(2)}) copy-start(bf16[8,32,256]{2,1,0:T(8,128)(2,1)} %x_ref.1) | copy-start | bytes 393220
  0.9 0.7 copy-start.15
  0.9 0.7 copy-start.16
  0.9 0.7 copy-start.18
  0.9 0.7 copy-start.19
  0.9 0.7 copy-start.20
  1.0 0.7 copy-start.14
  1.0 0.7 copy-start.17
  2.3 19.4 %copy-start.13 = (f32[16,1024]{1,0:T(8,128)S(1)}, f32[16,1024]{1,0:T(8,128)}, u32[]{:S(2)}) copy-start(f32[16,1024]{1,0:T(8,128)} %constant.5.clone.wave_ref) | copy-start | bytes 196612
  19.3 2.3 %copy-start.3 = (bf16[1024,128]{1,0:T(8,128)(2,1)S(1)}, bf16[1024,128]{1,0:T(8,128)(2,1)}, u32[]{:S(2)}) copy-start(bf16[1024,128]{1,0:T(8,128)(2,1)} %constant.4.clone.keyf_ref) | copy-start | bytes 786436
  19.3 2.3 %copy-start.5 = (bf16[256,256]{1,0:T(8,128)(2,1)S(1)}, bf16[256,256]{1,0:T(8,128)(2,1)}, u32[]{:S(2)}) copy-start(bf16[256,256]{1,0:T(8,128)(2,1)} %wq_ref.2) | copy-start | bytes 393220
  19.3 2.3 %copy-start.6 = (bf16[256,256]{1,0:T(8,128)(2,1)S(1)}, bf16[256,256]{1,0:T(8,128)(2,1)}, u32[]{:S(2)}) copy-start(bf16[256,256]{1,0:T(8,128)(2,1)} %wk_ref.2) | copy-start | bytes 393220
  19.3 2.4 %copy-start.7 = (bf16[256,256]{1,0:T(8,128)(2,1)S(1)}, bf16[256,256]{1,0:T(8,128)(2,1)}, u32[]{:S(2)}) copy-start(bf16[256,256]{1,0:T(8,128)(2,1)} %wv_ref.2) | copy-start | bytes 393220
  19.4 2.4 %copy-start.8 = (bf16[256,256]{1,0:T(8,128)(2,1)S(1)}, bf16[256,256]{1,0:T(8,128)(2,1)}, u32[]{:S(2)}) copy-start(bf16[256,256]{1,0:T(8,128)(2,1)} %wo_ref.2) | copy-start | bytes 393220
  21.7 37.6 %copy-start.1 = (bf16[256,1024]{1,0:T(8,128)(2,1)S(1)}, bf16[256,1024]{1,0:T(8,128)(2,1)}, u32[]{:S(2)}) copy-start(bf16[256,1024]{1,0:T(8,128)(2,1)} %wu_ref.1) | copy-start | bytes 1572868
  21.7 37.6 %copy-start.2 = (bf16[1024,256]{1,0:T(8,128)(2,1)S(1)}, bf16[1024,256]{1,0:T(8,128)(2,1)}, u32[]{:S(2)}) copy-start(bf16[1024,256]{1,0:T(8,128)(2,1)} %wd_ref.1) | copy-start | bytes 1572868
  21.7 37.6 %copy-start.9 = (bf16[256,256]{1,0:T(8,128)(2,1)S(1)}, bf16[256,256]{1,0:T(8,128)(2,1)}, u32[]{:S(2)}) copy-start(bf16[256,256]{1,0:T(8,128)(2,1)} %wq_ref.3) | copy-start | bytes 393220
  21.8 37.6 %copy-start.10 = (bf16[256,256]{1,0:T(8,128)(2,1)S(1)}, bf16[256,256]{1,0:T(8,128)(2,1)}, u32[]{:S(2)}) copy-start(bf16[256,256]{1,0:T(8,128)(2,1)} %wk_ref.3) | copy-start | bytes 393220
  21.8 37.6 %copy-start.11 = (bf16[256,256]{1,0:T(8,128)(2,1)S(1)}, bf16[256,256]{1,0:T(8,128)(2,1)}, u32[]{:S(2)}) copy-start(bf16[256,256]{1,0:T(8,128)(2,1)} %wv_ref.3) | copy-start | bytes 393220
  21.8 37.6 %copy-start.12 = (bf16[256,256]{1,0:T(8,128)(2,1)S(1)}, bf16[256,256]{1,0:T(8,128)(2,1)}, u32[]{:S(2)}) copy-start(bf16[256,256]{1,0:T(8,128)(2,1)} %wo_ref.3) | copy-start | bytes 393220
  25.7 33.7 %copy-start = (bf16[256,1024]{1,0:T(8,128)(2,1)S(1)}, bf16[256,1024]{1,0:T(8,128)(2,1)}, u32[]{:S(2)}) copy-start(bf16[256,1024]{1,0:T(8,128)(2,1)} %wg_ref.1) | copy-start | bytes 1572868

commit v4 on v3

--- a/solution.py
+++ b/solution.py
@@ -10,12 +10,11 @@
 from jax.sharding import Mesh
 from jax.sharding import PartitionSpec as P
 
-YA, YB, X, C, Z, YH = 2, 2, 4, 2, 8, 2
+YL, XA, XB, C, Z, YH = 4, 2, 2, 2, 8, 2
 HEADS, HEAD, D = 8, 32, 256
 F32, BF16 = jnp.float32, jnp.bfloat16
 LOG2E = 1.0 / math.log(2.0)
 VMEM = pl.BlockSpec(memory_space=pltpu.VMEM)
-SMEM = pl.BlockSpec(memory_space=pltpu.SMEM)
 PARAMS = pltpu.CompilerParams(vmem_limit_bytes=40 * 1024 * 1024)
 
 
@@ -29,30 +28,17 @@
 
 
 def twice_kernel(x_ref, out_ref):
-    for j in range(YA):
+    for j in range(XA):
         out_ref[j] = x_ref[...]
-
-
-def table_kernel(*refs):
-    gains, heads, table_ref = refs[:3], refs[3:7], refs[7]
-    for j, ref in enumerate(gains):
-        table_ref[j : j + 1, :] = ref[...]
-    root = 1.0 / math.sqrt(HEAD)
-    for h in range(HEADS):
-        rows = [jnp.full((1, D), ref[h], F32) for ref in heads]
-        table_ref[8 + h : 9 + h, :] = rows[1] / (rows[0] * root)
-        table_ref[16 + h : 17 + h, :] = rows[0] * (root * LOG2E)
-        table_ref[24 + h : 25 + h, :] = rows[2] * (root * LOG2E)
-        table_ref[32 + h : 33 + h, :] = rows[3] * LOG2E
 
 
 def row_kernel(
     x_ref, table_ref, wq_ref, wk_ref, wv_ref, wo_ref, keyf_ref, wave_ref,
     out_ref, norm_s, kext_s, att_s, first_s, send_s,
 ):
-    place = 2 * lax.axis_index("c") + lax.axis_index("ya")
+    place = 2 * lax.axis_index("c") + lax.axis_index("xa")
     own = pl.ds(pl.multiple_of(place * 256, 256), 256)
-    norm_s[...] = normed(x_ref[...].astype(F32), table_ref[0:1, :])
+    norm_s[...] = normed(x_ref[...].astype(F32), table_ref[32:33, :])
     keys = dot(norm_s[...], wk_ref[...]).astype(BF16)
     for g in range(2):
         kext_s[g, :, :128] = keys[:, 128 * g : 128 * g + 128]
@@ -65,7 +51,7 @@
 
     def scored(h):
         at = HEAD * (h % 4)
-        full = wave * table_ref[8 + h : 9 + h, :]
+        full = wave * table_ref[h : h + 1, :]
         high = full.astype(BF16).astype(F32)
         feats = jnp.where(low_rows, full - high, high).astype(BF16)
         parts = [qs_t[HEAD * h : HEAD * h + HEAD], feats, jnp.zeros((112, 256), BF16)]
@@ -93,7 +79,7 @@
         scores, peak = ahead
         if h + 1 < HEADS:
             ahead = scored(h + 1)
-        scale = table_ref[16 + h : 17 + h, :]
+        scale = table_ref[8 + h : 9 + h, :]
         expo = jnp.concatenate([jnp.exp2((s - peak) * scale).astype(BF16) for s in scores], axis=0)
         if behind is not None:
             mix(h - 1, behind)
@@ -120,7 +106,7 @@
         for f in range(2):
             first_s[k, :, 128 * f : 128 * f + 128] = wide_s[pl.ds(4 * f + k, 128, stride=8), :]
     for k in range(4):
-        norm_s[k] = normed(first_s[k], table_ref[1:2, :])
+        norm_s[k] = normed(first_s[k], table_ref[33:34, :])
     yh = lax.axis_index("yh")
     own = pl.ds(pl.multiple_of(yh * 64, 64), 64)
     flat = norm_s[...].reshape(512, D)
@@ -135,28 +121,33 @@
     spread = jnp.abs(lat_a - lat_b).astype(F32) * (1.0 / 128)
     head_of = lax.broadcasted_iota(jnp.int32, (64, D), 1) // HEAD
     mixes = []
-    for k in range(4):
+    def scored(k):
         q_one = qs[64 * k : 64 * k + 64]
         masked = jnp.concatenate([jnp.where(head_of == h, q_one, 0.0) for h in range(HEADS)], axis=0).astype(BF16)
-        raw = lax.dot_general(
+        return lax.dot_general(
             masked, keys[128 * k : 128 * k + 128], (((1,), (1,)), ((), ())), preferred_element_type=F32
         )
-        scores = jnp.concatenate(
-            [
-                raw[64 * h : 64 * h + 64] * table_ref[24 + h : 25 + h, :128] + spread * table_ref[32 + h : 33 + h, :128]
-                for h in range(HEADS)
-            ], axis=0
+
+    bias = jnp.concatenate([spread * table_ref[24 + h : 25 + h, :128] for h in range(HEADS)], axis=0)
+    raws = [scored(k) for k in range(4)]
+    expos = []
+    for k in range(4):
+        raw = raws[k]
+        scores = bias + jnp.concatenate(
+            [raw[64 * h : 64 * h + 64] * table_ref[16 + h : 17 + h, :128] for h in range(HEADS)], axis=0
         )
         expo = jnp.exp2(scores - jnp.max(scores, axis=-1, keepdims=True))
-        denom = jnp.sum(expo, axis=-1, keepdims=True)
-        mixed = dot(expo.astype(BF16), vals[128 * k : 128 * k + 128]) / denom
+        expos.append((expo.astype(BF16), jnp.sum(expo, axis=-1, keepdims=True)))
+    for k in range(4):
+        expo, denom = expos[k]
+        mixed = dot(expo, vals[128 * k : 128 * k + 128]) / denom
         total = jnp.where(head_of == 0, mixed[:64], 0.0)
         for h in range(1, HEADS):
             total = jnp.where(head_of == h, mixed[64 * h : 64 * h + 64], total)
         mixes.append(total.astype(BF16))
     resid = jnp.concatenate([first_s[k, own, :] for k in range(4)], axis=0)
     second = resid + dot(jnp.concatenate(mixes, axis=0), wo_ref[...])
-    third = normed(second, table_ref[2:3, :])
+    third = normed(second, table_ref[34:35, :])
     gate = dot(third, wg_ref[...])
     upper = dot(third, wu_ref[...])
     hidden = (gate / (1.0 + jnp.exp(-gate)) * upper).astype(BF16)
@@ -166,19 +157,24 @@
             out_ref[z, k] = updated[64 * k + 8 * z : 64 * k + 8 * z + 8].astype(BF16)
 
 
-def place_kernel(x_ref, out_ref, wide_s):
+def place_kernel(x_ref, out_ref, wide_s, done_s, sems):
     wide_s[0] = x_ref[:, :128].astype(F32)
     wide_s[1] = x_ref[:, 128:].astype(F32)
+    copies = []
     for row in range(8):
         parts = []
         for k in range(4):
             at = pl.ds(8 * k + row, 8, stride=32)
             parts.append(jnp.concatenate([wide_s[0, at, :], wide_s[1, at, :]], axis=1))
-        out_ref[row] = jnp.concatenate(parts, axis=0).astype(BF16)
+        done_s[row] = jnp.concatenate(parts, axis=0).astype(BF16)
+        copies.append(pltpu.make_async_copy(done_s.at[row], out_ref.at[row], sems.at[row]))
+        copies[-1].start()
+    for copy in copies:
+        copy.wait()
 
 
 def tables():
-    order = np.arange(1024).reshape(YA * YB * X, C, 32).transpose(1, 0, 2).reshape(1024)
+    order = np.arange(1024).reshape(YL, XA, XB, C, 32).transpose(3, 1, 0, 2, 4).reshape(1024)
     angle = order * (2.0 * math.pi / 1024)
     cos, sin = np.cos(angle), np.sin(angle)
     wave = np.zeros((16, 1024), np.float32)
@@ -197,24 +193,22 @@
     keyf, wave = tables()
     twice = pl.pallas_call(
         twice_kernel,
-        out_shape=jax.ShapeDtypeStruct((YA, 8, 32, D), BF16),
+        out_shape=jax.ShapeDtypeStruct((XA, 8, 32, D), BF16),
         in_specs=[VMEM],
         out_specs=VMEM,
         compiler_params=PARAMS,
     )(fields)
-    table = pl.pallas_call(
-        table_kernel,
-        out_shape=jax.ShapeDtypeStruct((40, D), F32),
-        in_specs=[VMEM] * 3 + [SMEM] * 4,
-        out_specs=VMEM,
-        compiler_params=PARAMS,
-    )(
-        norm_lon.reshape(1, D), norm_lat.reshape(1, D), norm_mlp.reshape(1, D),
-        temp_lon, bias_lon, temp_lat, bias_lat,
-    )
-    twice, table = lax.optimization_barrier((twice, table))
-    half = lax.all_to_all(twice.reshape(16, 32, D), ("ya", "yb", "x"), split_axis=0, concat_axis=0, tiled=True)
+    half = lax.all_to_all(twice.reshape(16, 32, D), ("xa", "yl", "xb"), split_axis=0, concat_axis=0, tiled=True)
     row = lax.all_gather(half, "c", axis=0, tiled=True)
+    row, temp_lon, bias_lon, temp_lat, bias_lat, norm_lon, norm_lat, norm_mlp = lax.optimization_barrier(
+        (row, temp_lon, bias_lon, temp_lat, bias_lat, norm_lon, norm_lat, norm_mlp)
+    )
+    scale_lon = temp_lon * (1.0 / math.sqrt(HEAD))
+    scale_lat = temp_lat * (1.0 / math.sqrt(HEAD))
+    values = jnp.stack([bias_lon / scale_lon, scale_lon * LOG2E, scale_lat * LOG2E, bias_lat * LOG2E])
+    table = jnp.concatenate(
+        [jnp.broadcast_to(values.reshape(32, 1), (32, D)), jnp.stack([norm_lon, norm_lat, norm_mlp])], axis=0
+    )
     sent = pl.pallas_call(
         row_kernel,
         out_shape=jax.ShapeDtypeStruct((2, 512, 128), BF16),
@@ -232,7 +226,7 @@
         row.reshape(1024, D), table, query_lon, key_lon, value_lon, out_lon, keyf, wave,
     )
     cols = lax.all_to_all(
-        sent.reshape(128, 8, 128), ("yh", "z", "yb", "x"), split_axis=0, concat_axis=0, tiled=True
+        sent.reshape(128, 8, 128), ("yh", "z", "yl", "xb"), split_axis=0, concat_axis=0, tiled=True
     )
     done = pl.pallas_call(
         col_kernel,
@@ -253,13 +247,13 @@
         place_kernel,
         out_shape=jax.ShapeDtypeStruct((8, 32, D), BF16),
         in_specs=[VMEM],
-        out_specs=VMEM,
-        scratch_shapes=[pltpu.VMEM((2, 256, 128), F32)],
+        out_specs=pl.BlockSpec(memory_space=pl.ANY),
+        scratch_shapes=[pltpu.VMEM((2, 256, 128), F32), pltpu.VMEM((8, 32, D), BF16), pltpu.SemaphoreType.DMA((8,))],
         compiler_params=PARAMS,
     )(home.reshape(256, D))
 
 
 def solution(mesh):
-    fine = Mesh(mesh.devices.reshape(YA, YB, X, C, Z, YH), ("ya", "yb", "x", "c", "z", "yh"))
-    cells = P(("z", "yh"), ("ya", "yb", "x", "c"), None)
+    fine = Mesh(mesh.devices.reshape(YL, XA, XB, C, Z, YH), ("yl", "xa", "xb", "c", "z", "yh"))
+    cells = P(("z", "yh"), ("yl", "xa", "xb", "c"), None)
     return jax.shard_map(body, mesh=fine, in_specs=(cells,) + (P(),) * 18, out_specs=cells, check_vma=False)

time: 74.2 us -> 70.9 us (0.956)
  the two profiles are of different devices: /device:TPU:8 before, /device:TPU:2 now
where the time goes in v4:
time: 70.9 us; the launch traced here: 70.6 us
  blocking collectives  61.7 us (87%)
  Pallas kernels  6.89 us (10%)
  local copies, waits for them, and re-layouts  1.65 us (2%)
    all_to_all x1, blocking collectives, body(): lax.all_to_all(sent.reshape(128, 8, 128), ('yh', 'z', 'yl', 'xb'), split_...  29.8 us
    all_to_all x1, blocking collectives, body(): lax.all_to_all(twice.reshape(16, 32, D), ('xa', 'yl', 'xb'), split_axis=0...  17.2 us
    all_to_all x1, blocking collectives, body(): lax.all_to_all(done.reshape(8, 32, D), 'z', split_axis=0, concat_axis=0,...  12.5 us
    pallas_call x1, Pallas kernels, body(): pl.pallas_call(row_kernel, out_shape=jax.ShapeDtypeStruct((2, 512, 128),...  3.89 us
    all_gather x1, blocking collectives, body(): row = lax.all_gather(half, 'c', axis=0, tiled=True)  2.31 us
    pallas_call x1, Pallas kernels, body(): pl.pallas_call(col_kernel, out_shape=jax.ShapeDtypeStruct((8, 4, 8, D), B...  2.13 us
    unnamed x42, local copies, waits for them, and re-layouts  1.56 us

profile of v4, /device:TPU:2, one launch (start us, length us, event | category | flops | bytes accessed | tf_op | source)
XLA Modules:
  0.0 70.6 jit_solution(6050947730144538545)
XLA Ops:
  0.0 0.0 copy-start.4
  0.0 0.9 %copy-done.4 = bf16[8,32,256]{2,1,0:T(8,128)(2,1)S(1)} copy-done((bf16[8,32,256]{2,1,0:T(8,128)(2,1)S(1)}, bf16[8,32,256]{2,1,0:T(8,128)(2,1)}, u32[]{:S(2)}) %copy-start.4) | copy-done | bytes 131096
  0.9 0.0 copy-start.17
  0.9 0.0 copy-start.18
  1.0 0.0 copy-start.19
  1.0 0.0 copy-start.20
  1.0 17.2 %all_to_all.15 = bf16[16,32,256]{2,1,0:T(8,128)(2,1)S(1)} all-to-all(bf16[16,32,256]{2,1,0:T(8,128)(2,1)S(1)} %bitcast.20), channel_id=1, replica_groups=mesh['yl'=4,'xa'=2,'xb'=2,'c'=2,'z'=8,'yh'=2] {'xa','yl','xb'}, dimensions={0} | all-to-all | bytes 524288 | tf_op jit(solution)/shard_map/all_to_all | solution.py:201
  18.1 0.0 copy-start.14
  18.1 0.0 copy-start.16
  18.1 0.0 copy-start.3
  18.1 0.0 copy-start.5
  18.2 0.0 copy-start.6
  18.2 0.0 copy-start.7
  18.2 0.0 copy-start.8
  18.2 2.3 %all_gather.3 = bf16[32,32,256]{2,1,0:T(8,128)(2,1)S(1)} all-gather(bf16[16,32,256]{2,1,0:T(8,128)(2,1)S(1)} %all_to_all.15), channel_id=1, replica_groups=mesh['yl'=4,'xa'=2,'xb'=2,'c'=2,'z'=8,'yh'=2] {'c'}, dimensions={0}, use_global_device_ids=true | all-gather | bytes 786432 | tf_op jit(solution)/shard_map/all_gather | solution.py:202
  20.5 0.0 copy-done.17
  20.5 0.0 copy-done.18
  20.5 0.0 copy-start.13
  20.5 0.0 copy-done.19
  20.5 0.0 copy-done.20
  20.6 0.1 reshape.26
  20.7 0.0 copy-done.14
  20.7 0.0 copy-done.15
  20.7 0.0 copy-done.16
  20.7 0.1 pad_maximum_fusion.table_ref
  20.8 0.0 copy-done.3
  20.8 0.0 copy-done.5
  20.8 0.0 copy-done.6
  20.8 0.0 copy-done.7
  20.8 0.0 copy-done.8
  20.8 0.6 copy-done.13
  21.4 0.0 copy-start.1
  21.4 0.0 copy-start.9
  21.4 0.0 copy-start.11
  21.4 0.0 copy-start.12
  21.4 3.9 %shard_map.200 = bf16[2,512,128]{2,1,0:T(8,128)(2,1)S(1)} custom-call(bf16[1024,256]{1,0:T(8,128)(2,1)S(1)} %bitcast.17, f32[35,256]{1,0:T(8,128)S(1)} %pad_maximum_fusion.table_ref, bf16[256,256]{1,0:T(8,128)(2,1)S(1)} %copy-done.5, bf16[256,256]{1,0:T(8,128)(2,1)S(1)} %copy-done.6, bf16[256,256]{1,0:T(8,128)(2,1)S(1)} %copy-done.7, ...), custom_call_target="tpu_custom_call" | custom-call | tf_op jit(solution)/shard_map/pallas_call | solution.py:212
  25.3 0.0 copy-start
  25.3 29.8 %all_to_all.16 = bf16[128,8,128]{2,1,0:T(8,128)(2,1)S(1)} all-to-all(bf16[128,8,128]{2,1,0:T(8,128)(2,1)S(1)} %bitcast.18), channel_id=1, replica_groups=mesh['yl'=4,'xa'=2,'xb'=2,'c'=2,'z'=8,'yh'=2] {'yh','z','yl','xb'}, dimensions={0} | all-to-all | bytes 524288 | tf_op jit(solution)/shard_map/all_to_all | solution.py:228
  55.1 0.0 copy-done.1
  55.1 0.0 copy-done.2
  55.1 0.0 copy-done.9
  55.1 0.0 copy-done.10
  55.1 0.0 copy-done.11
  55.1 0.0 copy-done.12
  55.1 0.0 copy-done
  55.1 2.1 %shard_map.201 = bf16[8,4,8,256]{3,2,1,0:T(8,128)(2,1)S(1)} custom-call(bf16[1024,128]{1,0:T(8,128)(2,1)S(1)} %bitcast.19, f32[35,256]{1,0:T(8,128)S(1)} %pad_maximum_fusion.table_ref, bf16[256,256]{1,0:T(8,128)(2,1)S(1)} %copy-done.9, bf16[256,256]{1,0:T(8,128)(2,1)S(1)} %copy-done.10, bf16[256,256]{1,0:T(8,128)(2,1)S(1)} %copy-done.11, ...), custom_call_target="tpu_custom_call" | custom-call | tf_op jit(solution)/shard_map/pallas_call | solution.py:231
  57.3 12.5 %all_to_all.17 = bf16[8,32,256]{2,1,0:T(8,128)(2,1)S(1)} all-to-all(bf16[8,32,256]{2,1,0:T(8,128)(2,1)S(1)} %bitcast.21), channel_id=1, replica_groups=mesh['yl'=4,'xa'=2,'xb'=2,'c'=2,'z'=8,'yh'=2] {'z'}, dimensions={0} | all-to-all | bytes 262144 | tf_op jit(solution)/shard_map/all_to_all | solution.py:245
  69.7 0.8 %shard_map.202 = bf16[8,32,256]{2,1,0:T(8,128)(2,1)} custom-call(bf16[256,256]{1,0:T(8,128)(2,1)S(1)} %bitcast.22), custom_call_target="tpu_custom_call" | custom-call | tf_op jit(solution)/shard_map/pallas_call | solution.py:246
  (8 shorter events, 0.1 us)
Async XLA Ops:
  0.0 0.9 %copy-start.4 = (bf16[8,32,256]{2,1,0:T(8,128)(2,1)S(1)}, bf16[8,32,256]{2,1,0:T(8,128)(2,1)}, u32[]{:S(2)}) copy-start(bf16[8,32,256]{2,1,0:T(8,128)(2,1)} %x_ref.1) | copy-start | bytes 393220
  0.9 19.6 %copy-start.17 = (f32[8]{0:T(128)S(1)}, f32[8]{0:T(128)}, u32[]{:S(2)}) copy-start(f32[8]{0:T(128)} %param.28) | copy-start | bytes 100
  0.9 19.6 %copy-start.18 = (f32[8]{0:T(128)S(1)}, f32[8]{0:T(128)}, u32[]{:S(2)}) copy-start(f32[8]{0:T(128)} %param.27) | copy-start | bytes 100
  1.0 19.6 %copy-start.19 = (f32[8]{0:T(128)S(1)}, f32[8]{0:T(128)}, u32[]{:S(2)}) copy-start(f32[8]{0:T(128)} %param.35) | copy-start | bytes 100
  1.0 19.6 %copy-start.20 = (f32[8]{0:T(128)S(1)}, f32[8]{0:T(128)}, u32[]{:S(2)}) copy-start(f32[8]{0:T(128)} %param.34) | copy-start | bytes 100
  18.1 2.5 %copy-start.14 = (f32[256]{0:T(256)S(1)}, f32[256]{0:T(256)}, u32[]{:S(2)}) copy-start(f32[256]{0:T(256)} %param.36) | copy-start | bytes 3076
  18.1 2.5 %copy-start.15 = (f32[256]{0:T(256)S(1)}, f32[256]{0:T(256)}, u32[]{:S(2)}) copy-start(f32[256]{0:T(256)} %param.29) | copy-start | bytes 3076
  18.1 2.5 %copy-start.16 = (f32[256]{0:T(256)S(1)}, f32[256]{0:T(256)}, u32[]{:S(2)}) copy-start(f32[256]{0:T(256)} %param.22) | copy-start | bytes 3076
  18.1 2.6 %copy-start.3 = (bf16[1024,128]{1,0:T(8,128)(2,1)S(1)}, bf16[1024,128]{1,0:T(8,128)(2,1)}, u32[]{:S(2)}) copy-start(bf16[1024,128]{1,0:T(8,128)(2,1)} %constant.11.clone.keyf_ref) | copy-start | bytes 786436
  18.1 2.6 %copy-start.5 = (bf16[256,256]{1,0:T(8,128)(2,1)S(1)}, bf16[256,256]{1,0:T(8,128)(2,1)}, u32[]{:S(2)}) copy-start(bf16[256,256]{1,0:T(8,128)(2,1)} %wq_ref.2) | copy-start | bytes 393220
  18.2 2.6 %copy-start.6 = (bf16[256,256]{1,0:T(8,128)(2,1)S(1)}, bf16[256,256]{1,0:T(8,128)(2,1)}, u32[]{:S(2)}) copy-start(bf16[256,256]{1,0:T(8,128)(2,1)} %wk_ref.2) | copy-start | bytes 393220
  18.2 2.6 %copy-start.7 = (bf16[256,256]{1,0:T(8,128)(2,1)S(1)}, bf16[256,256]{1,0:T(8,128)(2,1)}, u32[]{:S(2)}) copy-start(bf16[256,256]{1,0:T(8,128)(2,1)} %wv_ref.2) | copy-start | bytes 393220
  18.2 2.6 %copy-start.8 = (bf16[256,256]{1,0:T(8,128)(2,1)S(1)}, bf16[256,256]{1,0:T(8,128)(2,1)}, u32[]{:S(2)}) copy-start(bf16[256,256]{1,0:T(8,128)(2,1)} %wo_ref.2) | copy-start | bytes 393220
  20.5 0.8 %copy-start.13 = (f32[16,1024]{1,0:T(8,128)S(1)}, f32[16,1024]{1,0:T(8,128)}, u32[]{:S(2)}) copy-start(f32[16,1024]{1,0:T(8,128)} %constant.12.clone.wave_ref) | copy-start | bytes 196612
  21.4 33.7 %copy-start.1 = (bf16[256,1024]{1,0:T(8,128)(2,1)S(1)}, bf16[256,1024]{1,0:T(8,128)(2,1)}, u32[]{:S(2)}) copy-start(bf16[256,1024]{1,0:T(8,128)(2,1)} %wu_ref.1) | copy-start | bytes 1572868
  21.4 33.7 %copy-start.2 = (bf16[1024,256]{1,0:T(8,128)(2,1)S(1)}, bf16[1024,256]{1,0:T(8,128)(2,1)}, u32[]{:S(2)}) copy-start(bf16[1024,256]{1,0:T(8,128)(2,1)} %wd_ref.1) | copy-start | bytes 1572868
  21.4 33.7 %copy-start.9 = (bf16[256,256]{1,0:T(8,128)(2,1)S(1)}, bf16[256,256]{1,0:T(8,128)(2,1)}, u32[]{:S(2)}) copy-start(bf16[256,256]{1,0:T(8,128)(2,1)} %wq_ref.3) | copy-start | bytes 393220
  21.4 33.7 %copy-start.10 = (bf16[256,256]{1,0:T(8,128)(2,1)S(1)}, bf16[256,256]{1,0:T(8,128)(2,1)}, u32[]{:S(2)}) copy-start(bf16[256,256]{1,0:T(8,128)(2,1)} %wk_ref.3) | copy-start | bytes 393220
  21.4 33.7 %copy-start.11 = (bf16[256,256]{1,0:T(8,128)(2,1)S(1)}, bf16[256,256]{1,0:T(8,128)(2,1)}, u32[]{:S(2)}) copy-start(bf16[256,256]{1,0:T(8,128)(2,1)} %wv_ref.3) | copy-start | bytes 393220
  21.4 33.7 %copy-start.12 = (bf16[256,256]{1,0:T(8,128)(2,1)S(1)}, bf16[256,256]{1,0:T(8,128)(2,1)}, u32[]{:S(2)}) copy-start(bf16[256,256]{1,0:T(8,128)(2,1)} %wo_ref.3) | copy-start | bytes 393220
  25.3 29.8 %copy-start = (bf16[256,1024]{1,0:T(8,128)(2,1)S(1)}, bf16[256,1024]{1,0:T(8,128)(2,1)}, u32[]{:S(2)}) copy-start(bf16[256,1024]{1,0:T(8,128)(2,1)} %wg_ref.1) | copy-start | bytes 1572868

commit v5 on v4

--- a/solution.py
+++ b/solution.py
@@ -33,7 +33,7 @@
 
 
 def row_kernel(
-    x_ref, table_ref, wq_ref, wk_ref, wv_ref, wo_ref, keyf_ref, wave_ref,
+    x_ref, table_ref, wq_ref, wk_ref, wv_ref, wo_ref, keyf_ref,
     out_ref, norm_s, kext_s, att_s, first_s, send_s,
 ):
     place = 2 * lax.axis_index("c") + lax.axis_index("xa")
@@ -43,10 +43,11 @@
     for g in range(2):
         kext_s[g, :, :128] = keys[:, 128 * g : 128 * g + 128]
         kext_s[g, :, 128:] = keyf_ref[...]
-    vals_t = dot(norm_s[...], wv_ref[...]).T.astype(BF16)
-    qs_t = dot(norm_s[own, :], wq_ref[...]).T.astype(BF16)
-    wave = wave_ref[:, own]
-    low_rows = lax.broadcasted_iota(jnp.int32, wave.shape, 0) % 3 == 2
+    qs_t = dot(norm_s[own, :], wq_ref[...]).astype(BF16).T
+    turned = keyf_ref[own, :].astype(F32).T
+    at_row = lax.broadcasted_iota(jnp.int32, (16, 256), 0)
+    wave = jnp.where(at_row < 3, turned[0:1] + turned[1:2], jnp.where(at_row < 6, turned[3:4] + turned[4:5], 0.0))
+    low_rows = at_row % 3 == 2
     ones = jnp.ones((16, 1024), BF16)
 
     def scored(h):
@@ -72,15 +73,17 @@
 
     def mix(h, expo):
         mixed = dot(jnp.concatenate([vals_t[HEAD * h : HEAD * h + HEAD], ones], axis=0), expo)
-        att_s[HEAD * h : HEAD * h + HEAD, :] = mixed[:HEAD] / mixed[HEAD : HEAD + 1]
+        att_s[HEAD * h : HEAD * h + HEAD, :] = mixed[:HEAD] * (1.0 / mixed[HEAD : HEAD + 1])
 
     ahead, behind = scored(0), None
+    vals_t = dot(norm_s[...], wv_ref[...]).astype(BF16).T
     for h in range(HEADS):
         scores, peak = ahead
         if h + 1 < HEADS:
             ahead = scored(h + 1)
         scale = table_ref[8 + h : 9 + h, :]
-        expo = jnp.concatenate([jnp.exp2((s - peak) * scale).astype(BF16) for s in scores], axis=0)
+        lift = peak * scale
+        expo = jnp.concatenate([jnp.exp2(s * scale - lift).astype(BF16) for s in scores], axis=0)
         if behind is not None:
             mix(h - 1, behind)
         behind = expo
@@ -173,24 +176,21 @@
         copy.wait()
 
 
-def tables():
+def key_features():
     order = np.arange(1024).reshape(YL, XA, XB, C, 32).transpose(3, 1, 0, 2, 4).reshape(1024)
     angle = order * (2.0 * math.pi / 1024)
-    cos, sin = np.cos(angle), np.sin(angle)
-    wave = np.zeros((16, 1024), np.float32)
-    wave[0:3], wave[3:6] = cos, sin
     keyf = np.zeros((1024, 128), np.float32)
-    for at, v in ((0, cos), (3, sin)):
+    for at, v in ((0, np.cos(angle)), (3, np.sin(angle))):
         high = v.astype(jnp.bfloat16).astype(np.float64)
         keyf[:, at], keyf[:, at + 1], keyf[:, at + 2] = high, v - high, high
-    return keyf.astype(jnp.bfloat16), wave
+    return keyf.astype(jnp.bfloat16)
 
 
 def body(
     fields, norm_lon, query_lon, key_lon, value_lon, out_lon, temp_lon, bias_lon,
     norm_lat, query_lat, key_lat, value_lat, out_lat, temp_lat, bias_lat, norm_mlp, w_gate, w_up, w_down,
 ):
-    keyf, wave = tables()
+    keyf = key_features()
     twice = pl.pallas_call(
         twice_kernel,
         out_shape=jax.ShapeDtypeStruct((XA, 8, 32, D), BF16),
@@ -205,14 +205,14 @@
     )
     scale_lon = temp_lon * (1.0 / math.sqrt(HEAD))
     scale_lat = temp_lat * (1.0 / math.sqrt(HEAD))
-    values = jnp.stack([bias_lon / scale_lon, scale_lon * LOG2E, scale_lat * LOG2E, bias_lat * LOG2E])
+    rows = [bias_lon / scale_lon, scale_lon * LOG2E, scale_lat * LOG2E, bias_lat * LOG2E]
     table = jnp.concatenate(
-        [jnp.broadcast_to(values.reshape(32, 1), (32, D)), jnp.stack([norm_lon, norm_lat, norm_mlp])], axis=0
+        [jnp.broadcast_to(r.reshape(HEADS, 1), (HEADS, D)) for r in rows] + [jnp.stack([norm_lon, norm_lat, norm_mlp])], axis=0
     )
     sent = pl.pallas_call(
         row_kernel,
         out_shape=jax.ShapeDtypeStruct((2, 512, 128), BF16),
-        in_specs=[VMEM] * 8,
+        in_specs=[VMEM] * 7,
         out_specs=VMEM,
         scratch_shapes=[
             pltpu.VMEM((1024, D), BF16),
@@ -223,7 +223,7 @@
         ],
         compiler_params=PARAMS,
     )(
-        row.reshape(1024, D), table, query_lon, key_lon, value_lon, out_lon, keyf, wave,
+        row.reshape(1024, D), table, query_lon, key_lon, value_lon, out_lon, keyf,
     )
     cols = lax.all_to_all(
         sent.reshape(128, 8, 128), ("yh", "z", "yl", "xb"), split_axis=0, concat_axis=0, tiled=True

time: 70.9 us -> 70.5 us (level)
    unnamed x42 -> x40, local copies, waits for them, and re-layouts: 1.56 us -> 1.52 us
where the time goes in v5:
time: 70.5 us; the launch traced here: 70.3 us
  blocking collectives  61.6 us (87%)
  Pallas kernels  6.64 us (9%)
  local copies, waits for them, and re-layouts  1.82 us (3%)
    all_to_all x1, blocking collectives, body(): lax.all_to_all(sent.reshape(128, 8, 128), ('yh', 'z', 'yl', 'xb'), split_...  29.8 us
    all_to_all x1, blocking collectives, body(): lax.all_to_all(twice.reshape(16, 32, D), ('xa', 'yl', 'xb'), split_axis=0...  17 us
    all_to_all x1, blocking collectives, body(): lax.all_to_all(done.reshape(8, 32, D), 'z', split_axis=0, concat_axis=0,...  12.5 us
    pallas_call x1, Pallas kernels, body(): pl.pallas_call(row_kernel, out_shape=jax.ShapeDtypeStruct((2, 512, 128),...  3.65 us
    all_gather x1, blocking collectives, body(): row = lax.all_gather(half, 'c', axis=0, tiled=True)  2.31 us
    pallas_call x1, Pallas kernels, body(): pl.pallas_call(col_kernel, out_shape=jax.ShapeDtypeStruct((8, 4, 8, D), B...  2.13 us
    unnamed x40, local copies, waits for them, and re-layouts  1.52 us

profile of v5, /device:TPU:2, one launch (start us, length us, event | category | flops | bytes accessed | tf_op | source)
XLA Modules:
  0.0 70.3 jit_solution(17542114206471844504)
XLA Ops:
  0.0 0.0 copy-start.4
  0.0 0.9 %copy-done.4 = bf16[8,32,256]{2,1,0:T(8,128)(2,1)S(1)} copy-done((bf16[8,32,256]{2,1,0:T(8,128)(2,1)S(1)}, bf16[8,32,256]{2,1,0:T(8,128)(2,1)}, u32[]{:S(2)}) %copy-start.4) | copy-done | bytes 131096
  0.9 17.0 %all_to_all.15 = bf16[16,32,256]{2,1,0:T(8,128)(2,1)S(1)} all-to-all(bf16[16,32,256]{2,1,0:T(8,128)(2,1)S(1)} %bitcast.12), channel_id=1, replica_groups=mesh['yl'=4,'xa'=2,'xb'=2,'c'=2,'z'=8,'yh'=2] {'xa','yl','xb'}, dimensions={0} | all-to-all | bytes 524288 | tf_op jit(solution)/shard_map/all_to_all | solution.py:201
  18.0 0.0 copy-start.16
  18.0 0.0 copy-start.18
  18.0 0.0 copy-start.19
  18.0 0.0 copy-start.13
  18.0 0.0 copy-start.14
  18.0 0.0 copy-start.15
  18.0 0.0 copy-start.3
  18.0 0.0 copy-start.6
  18.0 0.0 copy-start.7
  18.0 0.0 copy-start.8
  18.1 2.3 %all_gather.3 = bf16[32,32,256]{2,1,0:T(8,128)(2,1)S(1)} all-gather(bf16[16,32,256]{2,1,0:T(8,128)(2,1)S(1)} %all_to_all.15), channel_id=1, replica_groups=mesh['yl'=4,'xa'=2,'xb'=2,'c'=2,'z'=8,'yh'=2] {'c'}, dimensions={0}, use_global_device_ids=true | all-gather | bytes 786432 | tf_op jit(solution)/shard_map/all_gather | solution.py:202
  20.4 0.0 copy-done.16
  20.4 0.0 copy-done.17
  20.4 0.0 copy-start.5
  20.4 0.0 copy-done.18
  20.4 0.0 copy-done.19
  20.4 0.1 broadcast_in_dim.11
  20.5 0.1 broadcast_in_dim.9
  20.6 0.1 broadcast_in_dim.10
  20.6 0.1 broadcast_in_dim.8
  20.7 0.0 copy-done.13
  20.7 0.0 copy-done.14
  20.7 0.0 copy-done.15
  20.7 0.0 copy-done.3
  20.7 0.0 copy-done.6
  20.7 0.0 copy-done.7
  20.8 0.0 copy-done.8
  20.8 0.5 copy-done.5
  21.3 0.0 copy-start.1
  21.3 0.0 copy-start.2
  21.3 0.0 copy-start.11
  21.3 0.0 copy-start.12
  21.3 3.6 %shard_map.191 = bf16[2,512,128]{2,1,0:T(8,128)(2,1)S(1)} custom-call(bf16[1024,256]{1,0:T(8,128)(2,1)S(1)} %bitcast.9, f32[35,256]{1,0:T(8,128)S(1)} %concatenate.3.table_ref, bf16[256,256]{1,0:T(8,128)(2,1)S(1)} %copy-done.5, bf16[256,256]{1,0:T(8,128)(2,1)S(1)} %copy-done.6, bf16[256,256]{1,0:T(8,128)(2,1)S(1)} %copy-done.7, ...), custom_call_target="tpu_custom_call" | custom-call | tf_op jit(solution)/shard_map/pallas_call | solution.py:212
  25.0 0.0 copy-start
  25.0 29.8 %all_to_all.16 = bf16[128,8,128]{2,1,0:T(8,128)(2,1)S(1)} all-to-all(bf16[128,8,128]{2,1,0:T(8,128)(2,1)S(1)} %bitcast.10), channel_id=1, replica_groups=mesh['yl'=4,'xa'=2,'xb'=2,'c'=2,'z'=8,'yh'=2] {'yh','z','yl','xb'}, dimensions={0} | all-to-all | bytes 524288 | tf_op jit(solution)/shard_map/all_to_all | solution.py:228
  54.7 0.0 copy-done.1
  54.7 0.0 copy-done.2
  54.7 0.0 copy-done.9
  54.7 0.0 copy-done.10
  54.8 0.0 copy-done.11
  54.8 0.0 copy-done.12
  54.8 0.0 copy-done
  54.8 2.1 %shard_map.192 = bf16[8,4,8,256]{3,2,1,0:T(8,128)(2,1)S(1)} custom-call(bf16[1024,128]{1,0:T(8,128)(2,1)S(1)} %bitcast.11, f32[35,256]{1,0:T(8,128)S(1)} %concatenate.3.table_ref, bf16[256,256]{1,0:T(8,128)(2,1)S(1)} %copy-done.9, bf16[256,256]{1,0:T(8,128)(2,1)S(1)} %copy-done.10, bf16[256,256]{1,0:T(8,128)(2,1)S(1)} %copy-done.11, ...), custom_call_target="tpu_custom_call" | custom-call | tf_op jit(solution)/shard_map/pallas_call | solution.py:231
  56.9 12.5 %all_to_all.17 = bf16[8,32,256]{2,1,0:T(8,128)(2,1)S(1)} all-to-all(bf16[8,32,256]{2,1,0:T(8,128)(2,1)S(1)} %bitcast.13), channel_id=1, replica_groups=mesh['yl'=4,'xa'=2,'xb'=2,'c'=2,'z'=8,'yh'=2] {'z'}, dimensions={0} | all-to-all | bytes 262144 | tf_op jit(solution)/shard_map/all_to_all | solution.py:245
  69.4 0.8 %shard_map.193 = bf16[8,32,256]{2,1,0:T(8,128)(2,1)} custom-call(bf16[256,256]{1,0:T(8,128)(2,1)S(1)} %bitcast.14), custom_call_target="tpu_custom_call" | custom-call | tf_op jit(solution)/shard_map/pallas_call | solution.py:246
  (7 shorter events, 0.1 us)
Async XLA Ops:
  0.0 0.9 %copy-start.4 = (bf16[8,32,256]{2,1,0:T(8,128)(2,1)S(1)}, bf16[8,32,256]{2,1,0:T(8,128)(2,1)}, u32[]{:S(2)}) copy-start(bf16[8,32,256]{2,1,0:T(8,128)(2,1)} %x_ref.1) | copy-start | bytes 393220
  18.0 2.4 %copy-start.16 = (f32[8]{0:T(128)S(1)}, f32[8]{0:T(128)}, u32[]{:S(2)}) copy-start(f32[8]{0:T(128)} %param.26) | copy-start | bytes 100
  18.0 2.4 %copy-start.17 = (f32[8]{0:T(128)S(1)}, f32[8]{0:T(128)}, u32[]{:S(2)}) copy-start(f32[8]{0:T(128)} %param.27) | copy-start | bytes 100
  18.0 2.4 %copy-start.18 = (f32[8]{0:T(128)S(1)}, f32[8]{0:T(128)}, u32[]{:S(2)}) copy-start(f32[8]{0:T(128)} %param.34) | copy-start | bytes 100
  18.0 2.4 %copy-start.19 = (f32[8]{0:T(128)S(1)}, f32[8]{0:T(128)}, u32[]{:S(2)}) copy-start(f32[8]{0:T(128)} %param.33) | copy-start | bytes 100
  18.0 2.7 %copy-start.13 = (f32[256]{0:T(256)S(1)}, f32[256]{0:T(256)}, u32[]{:S(2)}) copy-start(f32[256]{0:T(256)} %param.21) | copy-start | bytes 3076
  18.0 2.7 %copy-start.14 = (f32[256]{0:T(256)S(1)}, f32[256]{0:T(256)}, u32[]{:S(2)}) copy-start(f32[256]{0:T(256)} %param.28) | copy-start | bytes 3076
  18.0 2.7 %copy-start.15 = (f32[256]{0:T(256)S(1)}, f32[256]{0:T(256)}, u32[]{:S(2)}) copy-start(f32[256]{0:T(256)} %param.35) | copy-start | bytes 3076
  18.0 2.7 %copy-start.3 = (bf16[1024,128]{1,0:T(8,128)(2,1)S(1)}, bf16[1024,128]{1,0:T(8,128)(2,1)}, u32[]{:S(2)}) copy-start(bf16[1024,128]{1,0:T(8,128)(2,1)} %constant.9.clone.keyf_ref) | copy-start | bytes 786436
  18.0 2.7 %copy-start.6 = (bf16[256,256]{1,0:T(8,128)(2,1)S(1)}, bf16[256,256]{1,0:T(8,128)(2,1)}, u32[]{:S(2)}) copy-start(bf16[256,256]{1,0:T(8,128)(2,1)} %wk_ref.2) | copy-start | bytes 393220
  18.0 2.7 %copy-start.7 = (bf16[256,256]{1,0:T(8,128)(2,1)S(1)}, bf16[256,256]{1,0:T(8,128)(2,1)}, u32[]{:S(2)}) copy-start(bf16[256,256]{1,0:T(8,128)(2,1)} %wv_ref.2) | copy-start | bytes 393220
  18.0 2.7 %copy-start.8 = (bf16[256,256]{1,0:T(8,128)(2,1)S(1)}, bf16[256,256]{1,0:T(8,128)(2,1)}, u32[]{:S(2)}) copy-start(bf16[256,256]{1,0:T(8,128)(2,1)} %wo_ref.2) | copy-start | bytes 393220
  20.4 0.9 %copy-start.5 = (bf16[256,256]{1,0:T(8,128)(2,1)S(1)}, bf16[256,256]{1,0:T(8,128)(2,1)}, u32[]{:S(2)}) copy-start(bf16[256,256]{1,0:T(8,128)(2,1)} %wq_ref.2) | copy-start | bytes 393220
  21.3 33.5 %copy-start.1 = (bf16[256,1024]{1,0:T(8,128)(2,1)S(1)}, bf16[256,1024]{1,0:T(8,128)(2,1)}, u32[]{:S(2)}) copy-start(bf16[256,1024]{1,0:T(8,128)(2,1)} %wu_ref.1) | copy-start | bytes 1572868
  21.3 33.5 %copy-start.2 = (bf16[1024,256]{1,0:T(8,128)(2,1)S(1)}, bf16[1024,256]{1,0:T(8,128)(2,1)}, u32[]{:S(2)}) copy-start(bf16[1024,256]{1,0:T(8,128)(2,1)} %wd_ref.1) | copy-start | bytes 1572868
  21.3 33.5 %copy-start.9 = (bf16[256,256]{1,0:T(8,128)(2,1)S(1)}, bf16[256,256]{1,0:T(8,128)(2,1)}, u32[]{:S(2)}) copy-start(bf16[256,256]{1,0:T(8,128)(2,1)} %wq_ref.3) | copy-start | bytes 393220
  21.3 33.5 %copy-start.10 = (bf16[256,256]{1,0:T(8,128)(2,1)S(1)}, bf16[256,256]{1,0:T(8,128)(2,1)}, u32[]{:S(2)}) copy-start(bf16[256,256]{1,0:T(8,128)(2,1)} %wk_ref.3) | copy-start | bytes 393220
  21.3 33.5 %copy-start.11 = (bf16[256,256]{1,0:T(8,128)(2,1)S(1)}, bf16[256,256]{1,0:T(8,128)(2,1)}, u32[]{:S(2)}) copy-start(bf16[256,256]{1,0:T(8,128)(2,1)} %wv_ref.3) | copy-start | bytes 393220
  21.3 33.5 %copy-start.12 = (bf16[256,256]{1,0:T(8,128)(2,1)S(1)}, bf16[256,256]{1,0:T(8,128)(2,1)}, u32[]{:S(2)}) copy-start(bf16[256,256]{1,0:T(8,128)(2,1)} %wo_ref.3) | copy-start | bytes 393220
  25.0 29.8 %copy-start = (bf16[256,1024]{1,0:T(8,128)(2,1)S(1)}, bf16[256,1024]{1,0:T(8,128)(2,1)}, u32[]{:S(2)}) copy-start(bf16[256,1024]{1,0:T(8,128)(2,1)} %wg_ref.1) | copy-start | bytes 1572868

commit v6 on v5

--- a/solution.py
+++ b/solution.py
@@ -27,18 +27,32 @@
     return (values * factor * gain).astype(BF16)
 
 
+def by_head(ref):
+    at = [lax.broadcasted_iota(jnp.int32, (HEADS, HEADS), axis) for axis in range(2)]
+    picked = jnp.where(at[0] == at[1], jnp.broadcast_to(ref[...], (HEADS, HEADS)), 0.0)
+    return jnp.broadcast_to(jnp.sum(picked, axis=1, keepdims=True), (HEADS, D))
+
+
 def twice_kernel(x_ref, out_ref):
     for j in range(XA):
         out_ref[j] = x_ref[...]
 
 
 def row_kernel(
-    x_ref, table_ref, wq_ref, wk_ref, wv_ref, wo_ref, keyf_ref,
-    out_ref, norm_s, kext_s, att_s, first_s, send_s,
+    x_ref, gain_ref, gain2_ref, gain3_ref, temp_ref, bias_ref, temp2_ref, bias2_ref,
+    wq_ref, wk_ref, wv_ref, wo_ref, keyf_ref,
+    out_ref, next_ref, table_s, norm_s, kext_s, att_s, first_s, send_s,
 ):
     place = 2 * lax.axis_index("c") + lax.axis_index("xa")
     own = pl.ds(pl.multiple_of(place * 256, 256), 256)
-    norm_s[...] = normed(x_ref[...].astype(F32), table_ref[32:33, :])
+    scales = by_head(temp_ref) * (1.0 / math.sqrt(HEAD))
+    table_s[:HEADS] = by_head(bias_ref) / scales
+    table_s[HEADS:] = scales * LOG2E
+    next_ref[0:8] = by_head(temp2_ref) * (LOG2E / math.sqrt(HEAD))
+    next_ref[8:16] = by_head(bias2_ref) * LOG2E
+    next_ref[16:17] = gain2_ref[...]
+    next_ref[17:18] = gain3_ref[...]
+    norm_s[...] = normed(x_ref[...].astype(F32), gain_ref[...])
     keys = dot(norm_s[...], wk_ref[...]).astype(BF16)
     for g in range(2):
         kext_s[g, :, :128] = keys[:, 128 * g : 128 * g + 128]
@@ -52,7 +66,7 @@
 
     def scored(h):
         at = HEAD * (h % 4)
-        full = wave * table_ref[h : h + 1, :]
+        full = wave * table_s[h : h + 1, :]
         high = full.astype(BF16).astype(F32)
         feats = jnp.where(low_rows, full - high, high).astype(BF16)
         parts = [qs_t[HEAD * h : HEAD * h + HEAD], feats, jnp.zeros((112, 256), BF16)]
@@ -81,7 +95,7 @@
         scores, peak = ahead
         if h + 1 < HEADS:
             ahead = scored(h + 1)
-        scale = table_ref[8 + h : 9 + h, :]
+        scale = table_s[8 + h : 9 + h, :]
         lift = peak * scale
         expo = jnp.concatenate([jnp.exp2(s * scale - lift).astype(BF16) for s in scores], axis=0)
         if behind is not None:
@@ -109,7 +123,7 @@
         for f in range(2):
             first_s[k, :, 128 * f : 128 * f + 128] = wide_s[pl.ds(4 * f + k, 128, stride=8), :]
     for k in range(4):
-        norm_s[k] = normed(first_s[k], table_ref[33:34, :])
+        norm_s[k] = normed(first_s[k], table_ref[16:17, :])
     yh = lax.axis_index("yh")
     own = pl.ds(pl.multiple_of(yh * 64, 64), 64)
     flat = norm_s[...].reshape(512, D)
@@ -131,13 +145,13 @@
             masked, keys[128 * k : 128 * k + 128], (((1,), (1,)), ((), ())), preferred_element_type=F32
         )
 
-    bias = jnp.concatenate([spread * table_ref[24 + h : 25 + h, :128] for h in range(HEADS)], axis=0)
+    bias = jnp.concatenate([spread * table_ref[8 + h : 9 + h, :128] for h in range(HEADS)], axis=0)
     raws = [scored(k) for k in range(4)]
     expos = []
     for k in range(4):
         raw = raws[k]
         scores = bias + jnp.concatenate(
-            [raw[64 * h : 64 * h + 64] * table_ref[16 + h : 17 + h, :128] for h in range(HEADS)], axis=0
+            [raw[64 * h : 64 * h + 64] * table_ref[h : h + 1, :128] for h in range(HEADS)], axis=0
         )
         expo = jnp.exp2(scores - jnp.max(scores, axis=-1, keepdims=True))
         expos.append((expo.astype(BF16), jnp.sum(expo, axis=-1, keepdims=True)))
@@ -150,7 +164,7 @@
         mixes.append(total.astype(BF16))
     resid = jnp.concatenate([first_s[k, own, :] for k in range(4)], axis=0)
     second = resid + dot(jnp.concatenate(mixes, axis=0), wo_ref[...])
-    third = normed(second, table_ref[34:35, :])
+    third = normed(second, table_ref[17:18, :])
     gate = dot(third, wg_ref[...])
     upper = dot(third, wu_ref[...])
     hidden = (gate / (1.0 + jnp.exp(-gate)) * upper).astype(BF16)
@@ -160,20 +174,11 @@
             out_ref[z, k] = updated[64 * k + 8 * z : 64 * k + 8 * z + 8].astype(BF16)
 
 
-def place_kernel(x_ref, out_ref, wide_s, done_s, sems):
-    wide_s[0] = x_ref[:, :128].astype(F32)
-    wide_s[1] = x_ref[:, 128:].astype(F32)
-    copies = []
-    for row in range(8):
-        parts = []
-        for k in range(4):
-            at = pl.ds(8 * k + row, 8, stride=32)
-            parts.append(jnp.concatenate([wide_s[0, at, :], wide_s[1, at, :]], axis=1))
-        done_s[row] = jnp.concatenate(parts, axis=0).astype(BF16)
-        copies.append(pltpu.make_async_copy(done_s.at[row], out_ref.at[row], sems.at[row]))
-        copies[-1].start()
-    for copy in copies:
-        copy.wait()
+def place_kernel(x_ref, out_ref):
+    to = lax.broadcasted_iota(jnp.int32, (256, 256), 0)
+    source = 32 * (to % 8) + 8 * ((to // 8) % 4) + to // 32
+    moves = jnp.where(lax.broadcasted_iota(jnp.int32, (256, 256), 1) == source, 1.0, 0.0).astype(BF16)
+    out_ref[...] = dot(moves, x_ref[...]).astype(BF16).reshape(8, 32, D)
 
 
 def key_features():
@@ -200,21 +205,14 @@
     )(fields)
     half = lax.all_to_all(twice.reshape(16, 32, D), ("xa", "yl", "xb"), split_axis=0, concat_axis=0, tiled=True)
     row = lax.all_gather(half, "c", axis=0, tiled=True)
-    row, temp_lon, bias_lon, temp_lat, bias_lat, norm_lon, norm_lat, norm_mlp = lax.optimization_barrier(
-        (row, temp_lon, bias_lon, temp_lat, bias_lat, norm_lon, norm_lat, norm_mlp)
-    )
-    scale_lon = temp_lon * (1.0 / math.sqrt(HEAD))
-    scale_lat = temp_lat * (1.0 / math.sqrt(HEAD))
-    rows = [bias_lon / scale_lon, scale_lon * LOG2E, scale_lat * LOG2E, bias_lat * LOG2E]
-    table = jnp.concatenate(
-        [jnp.broadcast_to(r.reshape(HEADS, 1), (HEADS, D)) for r in rows] + [jnp.stack([norm_lon, norm_lat, norm_mlp])], axis=0
-    )
-    sent = pl.pallas_call(
+    row = row.reshape(1024, D)
+    sent, table = pl.pallas_call(
         row_kernel,
-        out_shape=jax.ShapeDtypeStruct((2, 512, 128), BF16),
-        in_specs=[VMEM] * 7,
-        out_specs=VMEM,
+        out_shape=(jax.ShapeDtypeStruct((2, 512, 128), BF16), jax.ShapeDtypeStruct((18, D), F32)),
+        in_specs=[VMEM] * 13,
+        out_specs=(VMEM, VMEM),
         scratch_shapes=[
+            pltpu.VMEM((2 * HEADS, D), F32),
             pltpu.VMEM((1024, D), BF16),
             pltpu.VMEM((2, 1024, D), BF16),
             pltpu.VMEM((D, 256), F32),
@@ -223,7 +221,8 @@
         ],
         compiler_params=PARAMS,
     )(
-        row.reshape(1024, D), table, query_lon, key_lon, value_lon, out_lon, keyf,
+        row, norm_lon.reshape(1, D), norm_lat.reshape(1, D), norm_mlp.reshape(1, D), temp_lon.reshape(1, HEADS),
+        bias_lon.reshape(1, HEADS), temp_lat.reshape(1, HEADS), bias_lat.reshape(1, HEADS), query_lon, key_lon, value_lon, out_lon, keyf,
     )
     cols = lax.all_to_all(
         sent.reshape(128, 8, 128), ("yh", "z", "yl", "xb"), split_axis=0, concat_axis=0, tiled=True
@@ -247,8 +246,7 @@
         place_kernel,
         out_shape=jax.ShapeDtypeStruct((8, 32, D), BF16),
         in_specs=[VMEM],
-        out_specs=pl.BlockSpec(memory_space=pl.ANY),
-        scratch_shapes=[pltpu.VMEM((2, 256, 128), F32), pltpu.VMEM((8, 32, D), BF16), pltpu.SemaphoreType.DMA((8,))],
+        out_specs=VMEM,
         compiler_params=PARAMS,
     )(home.reshape(256, D))
 

time: 70.5 us -> 70.4 us (level)
  no operation moved by 1% of the time
where the time goes in v6:
time: 70.4 us; the launch traced here: 70.2 us
  blocking collectives  61.7 us (88%)
  Pallas kernels  6.65 us (9%)
  local copies, waits for them, and re-layouts  1.58 us (2%)
    all_to_all x1, blocking collectives, body(): lax.all_to_all(sent.reshape(128, 8, 128), ('yh', 'z', 'yl', 'xb'), split_...  29.8 us
    all_to_all x1, blocking collectives, body(): lax.all_to_all(twice.reshape(16, 32, D), ('xa', 'yl', 'xb'), split_axis=0...  17.2 us
    all_to_all x1, blocking collectives, body(): lax.all_to_all(done.reshape(8, 32, D), 'z', split_axis=0, concat_axis=0,...  12.5 us
    pallas_call x1, Pallas kernels, body(): pl.pallas_call(row_kernel, out_shape=(jax.ShapeDtypeStruct((2, 512, 128),...  3.66 us
    all_gather x1, blocking collectives, body(): row = lax.all_gather(half, 'c', axis=0, tiled=True)  2.31 us
    pallas_call x1, Pallas kernels, body(): pl.pallas_call(col_kernel, out_shape=jax.ShapeDtypeStruct((8, 4, 8, D), B...  2.13 us
    unnamed x40, local copies, waits for them, and re-layouts  1.58 us

profile of v6, /device:TPU:2, one launch (start us, length us, event | category | flops | bytes accessed | tf_op | source)
XLA Modules:
  0.0 70.2 jit_solution(2004178346026463444)
XLA Ops:
  0.0 0.0 copy-start.4
  0.0 0.9 %copy-done.4 = bf16[8,32,256]{2,1,0:T(8,128)(2,1)S(1)} copy-done((bf16[8,32,256]{2,1,0:T(8,128)(2,1)S(1)}, bf16[8,32,256]{2,1,0:T(8,128)(2,1)}, u32[]{:S(2)}) %copy-start.4) | copy-done | bytes 131096
  0.9 0.0 copy-start.11
  0.9 0.0 copy-start.12
  1.0 17.2 %all_to_all.15 = bf16[16,32,256]{2,1,0:T(8,128)(2,1)S(1)} all-to-all(bf16[16,32,256]{2,1,0:T(8,128)(2,1)S(1)} %bitcast.15), channel_id=1, replica_groups=mesh['yl'=4,'xa'=2,'xb'=2,'c'=2,'z'=8,'yh'=2] {'xa','yl','xb'}, dimensions={0} | all-to-all | bytes 524288 | tf_op jit(solution)/shard_map/all_to_all | solution.py:206
  18.1 0.0 copy-start.3
  18.1 0.0 copy-start.5
  18.1 0.0 copy-start.6
  18.1 0.0 copy-start.7
  18.1 0.0 copy-start.8
  18.1 0.0 copy-start.14
  18.1 0.0 copy-start.15
  18.2 0.0 copy-start.17
  18.2 0.0 copy-start.18
  18.2 0.0 copy-start.19
  18.2 2.3 %all_gather.3 = bf16[32,32,256]{2,1,0:T(8,128)(2,1)S(1)} all-gather(bf16[16,32,256]{2,1,0:T(8,128)(2,1)S(1)} %all_to_all.15), channel_id=1, replica_groups=mesh['yl'=4,'xa'=2,'xb'=2,'c'=2,'z'=8,'yh'=2] {'c'}, dimensions={0}, use_global_device_ids=true | all-gather | bytes 786432 | tf_op jit(solution)/shard_map/all_gather | solution.py:207
  20.5 0.0 copy-start.13
  20.5 0.0 copy-start.16
  20.5 0.0 copy-done.3
  20.5 0.0 copy-done.5
  20.5 0.0 copy-done.6
  20.5 0.0 copy-done.7
  20.5 0.0 copy-done.8
  20.6 0.0 copy-done.14
  20.6 0.0 copy-done.15
  20.6 0.0 copy-done.17
  20.6 0.0 copy-done.18
  20.6 0.0 copy-done.19
  20.6 0.6 copy-done.13
  21.2 0.0 copy-done.16
  21.2 0.0 copy-start.1
  21.2 0.0 copy-start.2
  21.2 0.0 copy-start.9
  21.2 0.0 copy-start.10
  21.2 3.7 %shard_map.191 = (bf16[2,512,128]{2,1,0:T(8,128)(2,1)S(1)}, f32[18,256]{1,0:T(8,128)S(1)}) custom-call(bf16[1024,256]{1,0:T(8,128)(2,1)S(1)} %bitcast.13, f32[1,256]{1,0:T(1,128)S(1)} %bitcast.19, f32[1,256]{1,0:T(1,128)S(1)} %bitcast.20, f32[1,256]{1,0:T(1,128)S(1)} %bitcast.21, f32[1,8]{1,0:T(1,128)S(1)} %bitcast.22, f32[1,8]{1,0:T(1,128)S(1)} %bitcast.23, ...), custom_call_target="tpu_custom_call" | custom-call | tf_op jit(solution)/shard_map/pallas_call | solution.py:209
  24.9 0.0 copy-start
  24.9 29.8 %all_to_all.16 = bf16[128,8,128]{2,1,0:T(8,128)(2,1)S(1)} all-to-all(bf16[128,8,128]{2,1,0:T(8,128)(2,1)S(1)} %bitcast.18), channel_id=1, replica_groups=mesh['yl'=4,'xa'=2,'xb'=2,'c'=2,'z'=8,'yh'=2] {'yh','z','yl','xb'}, dimensions={0} | all-to-all | bytes 524288 | tf_op jit(solution)/shard_map/all_to_all | solution.py:227
  54.6 0.0 copy-done.11
  54.6 0.0 copy-done.12
  54.6 0.0 copy-done.1
  54.7 0.0 copy-done.2
  54.7 0.0 copy-done.9
  54.7 0.0 copy-done.10
  54.7 0.0 copy-done
  54.7 2.1 %shard_map.192 = bf16[8,4,8,256]{3,2,1,0:T(8,128)(2,1)S(1)} custom-call(bf16[1024,128]{1,0:T(8,128)(2,1)S(1)} %bitcast.14, f32[18,256]{1,0:T(8,128)S(1)} %get-tuple-element.8.table_ref, bf16[256,256]{1,0:T(8,128)(2,1)S(1)} %copy-done.9, bf16[256,256]{1,0:T(8,128)(2,1)S(1)} %copy-done.10, bf16[256,256]{1,0:T(8,128)(2,1)S(1)} %copy-done.11, ...), custom_call_target="tpu_custom_call" | custom-call | tf_op jit(solution)/shard_map/pallas_call | solution.py:230
  56.8 12.5 %all_to_all.17 = bf16[8,32,256]{2,1,0:T(8,128)(2,1)S(1)} all-to-all(bf16[8,32,256]{2,1,0:T(8,128)(2,1)S(1)} %bitcast.16), channel_id=1, replica_groups=mesh['yl'=4,'xa'=2,'xb'=2,'c'=2,'z'=8,'yh'=2] {'z'}, dimensions={0} | all-to-all | bytes 262144 | tf_op jit(solution)/shard_map/all_to_all | solution.py:244
  69.3 0.8 %shard_map.193 = bf16[8,32,256]{2,1,0:T(8,128)(2,1)} custom-call(bf16[256,256]{1,0:T(8,128)(2,1)S(1)} %bitcast.17), custom_call_target="tpu_custom_call" | custom-call | tf_op jit(solution)/shard_map/pallas_call | solution.py:245
  (1 shorter events, 0.0 us)
Async XLA Ops:
  0.0 0.9 %copy-start.4 = (bf16[8,32,256]{2,1,0:T(8,128)(2,1)S(1)}, bf16[8,32,256]{2,1,0:T(8,128)(2,1)}, u32[]{:S(2)}) copy-start(bf16[8,32,256]{2,1,0:T(8,128)(2,1)} %x_ref.1) | copy-start | bytes 393220
  0.9 53.7 %copy-start.11 = (bf16[256,256]{1,0:T(8,128)(2,1)S(1)}, bf16[256,256]{1,0:T(8,128)(2,1)}, u32[]{:S(2)}) copy-start(bf16[256,256]{1,0:T(8,128)(2,1)} %wv_ref.3) | copy-start | bytes 393220
  0.9 53.7 %copy-start.12 = (bf16[256,256]{1,0:T(8,128)(2,1)S(1)}, bf16[256,256]{1,0:T(8,128)(2,1)}, u32[]{:S(2)}) copy-start(bf16[256,256]{1,0:T(8,128)(2,1)} %wo_ref.3) | copy-start | bytes 393220
  18.1 2.4 %copy-start.3 = (bf16[1024,128]{1,0:T(8,128)(2,1)S(1)}, bf16[1024,128]{1,0:T(8,128)(2,1)}, u32[]{:S(2)}) copy-start(bf16[1024,128]{1,0:T(8,128)(2,1)} %constant.2.clone.keyf_ref) | copy-start | bytes 786436
  18.1 2.4 %copy-start.5 = (bf16[256,256]{1,0:T(8,128)(2,1)S(1)}, bf16[256,256]{1,0:T(8,128)(2,1)}, u32[]{:S(2)}) copy-start(bf16[256,256]{1,0:T(8,128)(2,1)} %wq_ref.2) | copy-start | bytes 393220
  18.1 2.4 %copy-start.6 = (bf16[256,256]{1,0:T(8,128)(2,1)S(1)}, bf16[256,256]{1,0:T(8,128)(2,1)}, u32[]{:S(2)}) copy-start(bf16[256,256]{1,0:T(8,128)(2,1)} %wk_ref.2) | copy-start | bytes 393220
  18.1 2.4 %copy-start.7 = (bf16[256,256]{1,0:T(8,128)(2,1)S(1)}, bf16[256,256]{1,0:T(8,128)(2,1)}, u32[]{:S(2)}) copy-start(bf16[256,256]{1,0:T(8,128)(2,1)} %wv_ref.2) | copy-start | bytes 393220
  18.1 2.4 %copy-start.8 = (bf16[256,256]{1,0:T(8,128)(2,1)S(1)}, bf16[256,256]{1,0:T(8,128)(2,1)}, u32[]{:S(2)}) copy-start(bf16[256,256]{1,0:T(8,128)(2,1)} %wo_ref.2) | copy-start | bytes 393220
  18.1 2.4 %copy-start.14 = (f32[256]{0:T(256)S(1)}, f32[256]{0:T(256)}, u32[]{:S(2)}) copy-start(f32[256]{0:T(256)} %param.28) | copy-start | bytes 3076
  18.1 2.4 %copy-start.15 = (f32[256]{0:T(256)S(1)}, f32[256]{0:T(256)}, u32[]{:S(2)}) copy-start(f32[256]{0:T(256)} %param.35) | copy-start | bytes 3076
  18.2 2.4 %copy-start.17 = (f32[8]{0:T(128)S(1)}, f32[8]{0:T(128)}, u32[]{:S(2)}) copy-start(f32[8]{0:T(128)} %param.27) | copy-start | bytes 100
  18.2 2.4 %copy-start.18 = (f32[8]{0:T(128)S(1)}, f32[8]{0:T(128)}, u32[]{:S(2)}) copy-start(f32[8]{0:T(128)} %param.33) | copy-start | bytes 100
  18.2 2.4 %copy-start.19 = (f32[8]{0:T(128)S(1)}, f32[8]{0:T(128)}, u32[]{:S(2)}) copy-start(f32[8]{0:T(128)} %param.34) | copy-start | bytes 100
  20.5 0.7 copy-start.13
  20.5 0.7 copy-start.16
  21.2 33.5 %copy-start.1 = (bf16[256,1024]{1,0:T(8,128)(2,1)S(1)}, bf16[256,1024]{1,0:T(8,128)(2,1)}, u32[]{:S(2)}) copy-start(bf16[256,1024]{1,0:T(8,128)(2,1)} %wu_ref.1) | copy-start | bytes 1572868
  21.2 33.5 %copy-start.2 = (bf16[1024,256]{1,0:T(8,128)(2,1)S(1)}, bf16[1024,256]{1,0:T(8,128)(2,1)}, u32[]{:S(2)}) copy-start(bf16[1024,256]{1,0:T(8,128)(2,1)} %wd_ref.1) | copy-start | bytes 1572868
  21.2 33.5 %copy-start.9 = (bf16[256,256]{1,0:T(8,128)(2,1)S(1)}, bf16[256,256]{1,0:T(8,128)(2,1)}, u32[]{:S(2)}) copy-start(bf16[256,256]{1,0:T(8,128)(2,1)} %wq_ref.3) | copy-start | bytes 393220
  21.2 33.5 %copy-start.10 = (bf16[256,256]{1,0:T(8,128)(2,1)S(1)}, bf16[256,256]{1,0:T(8,128)(2,1)}, u32[]{:S(2)}) copy-start(bf16[256,256]{1,0:T(8,128)(2,1)} %wk_ref.3) | copy-start | bytes 393220
  24.9 29.8 %copy-start = (bf16[256,1024]{1,0:T(8,128)(2,1)S(1)}, bf16[256,1024]{1,0:T(8,128)(2,1)}, u32[]{:S(2)}) copy-start(bf16[256,1024]{1,0:T(8,128)(2,1)} %wg_ref.1) | copy-start | bytes 1572868

commit v7 on v6

--- a/solution.py
+++ b/solution.py
@@ -130,7 +130,7 @@
     keys = dot(flat, wk_ref[...]).astype(BF16)
     vals = dot(flat, wv_ref[...]).astype(BF16)
     mine = jnp.concatenate([norm_s[k, own, :] for k in range(4)], axis=0)
-    qs = dot(mine, wq_ref[...])
+    qs = dot(mine, wq_ref[...]).astype(BF16)
     a = lax.broadcasted_iota(jnp.int32, (64, 128), 0)
     b = lax.broadcasted_iota(jnp.int32, (64, 128), 1)
     lat_a = 16 * (a // 8) + 8 * yh + a % 8
@@ -140,7 +140,7 @@
     mixes = []
     def scored(k):
         q_one = qs[64 * k : 64 * k + 64]
-        masked = jnp.concatenate([jnp.where(head_of == h, q_one, 0.0) for h in range(HEADS)], axis=0).astype(BF16)
+        masked = jnp.concatenate([jnp.where(head_of == h, q_one, 0.0).astype(BF16) for h in range(HEADS)], axis=0)
         return lax.dot_general(
             masked, keys[128 * k : 128 * k + 128], (((1,), (1,)), ((), ())), preferred_element_type=F32
         )
@@ -165,10 +165,12 @@
     resid = jnp.concatenate([first_s[k, own, :] for k in range(4)], axis=0)
     second = resid + dot(jnp.concatenate(mixes, axis=0), wo_ref[...])
     third = normed(second, table_ref[17:18, :])
-    gate = dot(third, wg_ref[...])
-    upper = dot(third, wu_ref[...])
-    hidden = (gate / (1.0 + jnp.exp(-gate)) * upper).astype(BF16)
-    updated = second + dot(hidden, wd_ref[...])
+    updated = second
+    for at in range(0, 1024, 256):
+        gate = dot(third, wg_ref[:, at : at + 256])
+        upper = dot(third, wu_ref[:, at : at + 256])
+        hidden = (gate / (1.0 + jnp.exp(-gate)) * upper).astype(BF16)
+        updated = updated + dot(hidden, wd_ref[at : at + 256, :])
     for k in range(4):
         for z in range(8):
             out_ref[z, k] = updated[64 * k + 8 * z : 64 * k + 8 * z + 8].astype(BF16)

time: 70.4 us -> 70.4 us (level)
  no operation moved by 1% of the time
where the time goes in v7:
time: 70.4 us; the launch traced here: 70.2 us
  blocking collectives  61.7 us (88%)
  Pallas kernels  6.66 us (9%)
  local copies, waits for them, and re-layouts  1.58 us (2%)
    all_to_all x1, blocking collectives, body(): lax.all_to_all(sent.reshape(128, 8, 128), ('yh', 'z', 'yl', 'xb'), split_...  29.8 us
    all_to_all x1, blocking collectives, body(): lax.all_to_all(twice.reshape(16, 32, D), ('xa', 'yl', 'xb'), split_axis=0...  17.2 us
    all_to_all x1, blocking collectives, body(): lax.all_to_all(done.reshape(8, 32, D), 'z', split_axis=0, concat_axis=0,...  12.5 us
    pallas_call x1, Pallas kernels, body(): pl.pallas_call(row_kernel, out_shape=(jax.ShapeDtypeStruct((2, 512, 128),...  3.66 us
    all_gather x1, blocking collectives, body(): row = lax.all_gather(half, 'c', axis=0, tiled=True)  2.31 us
    pallas_call x1, Pallas kernels, body(): pl.pallas_call(col_kernel, out_shape=jax.ShapeDtypeStruct((8, 4, 8, D), B...  2.13 us
    unnamed x40, local copies, waits for them, and re-layouts  1.58 us

profile of v7, /device:TPU:2, one launch (start us, length us, event | category | flops | bytes accessed | tf_op | source)
XLA Modules:
  0.0 70.2 jit_solution(9814146185659048049)
XLA Ops:
  0.0 0.0 copy-start.4
  0.0 0.9 %copy-done.4 = bf16[8,32,256]{2,1,0:T(8,128)(2,1)S(1)} copy-done((bf16[8,32,256]{2,1,0:T(8,128)(2,1)S(1)}, bf16[8,32,256]{2,1,0:T(8,128)(2,1)}, u32[]{:S(2)}) %copy-start.4) | copy-done | bytes 131096
  0.9 0.0 copy-start.11
  0.9 0.0 copy-start.12
  1.0 17.2 %all_to_all.15 = bf16[16,32,256]{2,1,0:T(8,128)(2,1)S(1)} all-to-all(bf16[16,32,256]{2,1,0:T(8,128)(2,1)S(1)} %bitcast.15), channel_id=1, replica_groups=mesh['yl'=4,'xa'=2,'xb'=2,'c'=2,'z'=8,'yh'=2] {'xa','yl','xb'}, dimensions={0} | all-to-all | bytes 524288 | tf_op jit(solution)/shard_map/all_to_all | solution.py:208
  18.1 0.0 copy-start.3
  18.1 0.0 copy-start.5
  18.1 0.0 copy-start.6
  18.1 0.0 copy-start.7
  18.1 0.0 copy-start.8
  18.1 0.0 copy-start.14
  18.1 0.0 copy-start.15
  18.2 0.0 copy-start.17
  18.2 0.0 copy-start.18
  18.2 0.0 copy-start.19
  18.2 2.3 %all_gather.3 = bf16[32,32,256]{2,1,0:T(8,128)(2,1)S(1)} all-gather(bf16[16,32,256]{2,1,0:T(8,128)(2,1)S(1)} %all_to_all.15), channel_id=1, replica_groups=mesh['yl'=4,'xa'=2,'xb'=2,'c'=2,'z'=8,'yh'=2] {'c'}, dimensions={0}, use_global_device_ids=true | all-gather | bytes 786432 | tf_op jit(solution)/shard_map/all_gather | solution.py:209
  20.5 0.0 copy-start.13
  20.5 0.0 copy-start.16
  20.5 0.0 copy-done.3
  20.5 0.0 copy-done.5
  20.5 0.0 copy-done.6
  20.5 0.0 copy-done.7
  20.5 0.0 copy-done.8
  20.6 0.0 copy-done.14
  20.6 0.0 copy-done.15
  20.6 0.0 copy-done.17
  20.6 0.0 copy-done.18
  20.6 0.0 copy-done.19
  20.6 0.6 copy-done.13
  21.2 0.0 copy-done.16
  21.2 0.0 copy-start.1
  21.2 0.0 copy-start.2
  21.2 0.0 copy-start.9
  21.2 0.0 copy-start.10
  21.2 3.7 %shard_map.191 = (bf16[2,512,128]{2,1,0:T(8,128)(2,1)S(1)}, f32[18,256]{1,0:T(8,128)S(1)}) custom-call(bf16[1024,256]{1,0:T(8,128)(2,1)S(1)} %bitcast.13, f32[1,256]{1,0:T(1,128)S(1)} %bitcast.19, f32[1,256]{1,0:T(1,128)S(1)} %bitcast.20, f32[1,256]{1,0:T(1,128)S(1)} %bitcast.21, f32[1,8]{1,0:T(1,128)S(1)} %bitcast.22, f32[1,8]{1,0:T(1,128)S(1)} %bitcast.23, ...), custom_call_target="tpu_custom_call" | custom-call | tf_op jit(solution)/shard_map/pallas_call | solution.py:211
  24.9 0.0 copy-start
  24.9 29.8 %all_to_all.16 = bf16[128,8,128]{2,1,0:T(8,128)(2,1)S(1)} all-to-all(bf16[128,8,128]{2,1,0:T(8,128)(2,1)S(1)} %bitcast.18), channel_id=1, replica_groups=mesh['yl'=4,'xa'=2,'xb'=2,'c'=2,'z'=8,'yh'=2] {'yh','z','yl','xb'}, dimensions={0} | all-to-all | bytes 524288 | tf_op jit(solution)/shard_map/all_to_all | solution.py:229
  54.6 0.0 copy-done.11
  54.6 0.0 copy-done.12
  54.6 0.0 copy-done.1
  54.7 0.0 copy-done.2
  54.7 0.0 copy-done.9
  54.7 0.0 copy-done.10
  54.7 0.0 copy-done
  54.7 2.1 %shard_map.192 = bf16[8,4,8,256]{3,2,1,0:T(8,128)(2,1)S(1)} custom-call(bf16[1024,128]{1,0:T(8,128)(2,1)S(1)} %bitcast.14, f32[18,256]{1,0:T(8,128)S(1)} %get-tuple-element.8.table_ref, bf16[256,256]{1,0:T(8,128)(2,1)S(1)} %copy-done.9, bf16[256,256]{1,0:T(8,128)(2,1)S(1)} %copy-done.10, bf16[256,256]{1,0:T(8,128)(2,1)S(1)} %copy-done.11, ...), custom_call_target="tpu_custom_call" | custom-call | tf_op jit(solution)/shard_map/pallas_call | solution.py:232
  56.8 12.5 %all_to_all.17 = bf16[8,32,256]{2,1,0:T(8,128)(2,1)S(1)} all-to-all(bf16[8,32,256]{2,1,0:T(8,128)(2,1)S(1)} %bitcast.16), channel_id=1, replica_groups=mesh['yl'=4,'xa'=2,'xb'=2,'c'=2,'z'=8,'yh'=2] {'z'}, dimensions={0} | all-to-all | bytes 262144 | tf_op jit(solution)/shard_map/all_to_all | solution.py:246
  69.3 0.8 %shard_map.193 = bf16[8,32,256]{2,1,0:T(8,128)(2,1)} custom-call(bf16[256,256]{1,0:T(8,128)(2,1)S(1)} %bitcast.17), custom_call_target="tpu_custom_call" | custom-call | tf_op jit(solution)/shard_map/pallas_call | solution.py:247
  (1 shorter events, 0.0 us)
Async XLA Ops:
  0.0 0.9 %copy-start.4 = (bf16[8,32,256]{2,1,0:T(8,128)(2,1)S(1)}, bf16[8,32,256]{2,1,0:T(8,128)(2,1)}, u32[]{:S(2)}) copy-start(bf16[8,32,256]{2,1,0:T(8,128)(2,1)} %x_ref.1) | copy-start | bytes 393220
  0.9 53.7 %copy-start.11 = (bf16[256,256]{1,0:T(8,128)(2,1)S(1)}, bf16[256,256]{1,0:T(8,128)(2,1)}, u32[]{:S(2)}) copy-start(bf16[256,256]{1,0:T(8,128)(2,1)} %wv_ref.3) | copy-start | bytes 393220
  0.9 53.7 %copy-start.12 = (bf16[256,256]{1,0:T(8,128)(2,1)S(1)}, bf16[256,256]{1,0:T(8,128)(2,1)}, u32[]{:S(2)}) copy-start(bf16[256,256]{1,0:T(8,128)(2,1)} %wo_ref.3) | copy-start | bytes 393220
  18.1 2.4 %copy-start.3 = (bf16[1024,128]{1,0:T(8,128)(2,1)S(1)}, bf16[1024,128]{1,0:T(8,128)(2,1)}, u32[]{:S(2)}) copy-start(bf16[1024,128]{1,0:T(8,128)(2,1)} %constant.2.clone.keyf_ref) | copy-start | bytes 786436
  18.1 2.4 %copy-start.5 = (bf16[256,256]{1,0:T(8,128)(2,1)S(1)}, bf16[256,256]{1,0:T(8,128)(2,1)}, u32[]{:S(2)}) copy-start(bf16[256,256]{1,0:T(8,128)(2,1)} %wq_ref.2) | copy-start | bytes 393220
  18.1 2.4 %copy-start.6 = (bf16[256,256]{1,0:T(8,128)(2,1)S(1)}, bf16[256,256]{1,0:T(8,128)(2,1)}, u32[]{:S(2)}) copy-start(bf16[256,256]{1,0:T(8,128)(2,1)} %wk_ref.2) | copy-start | bytes 393220
  18.1 2.4 %copy-start.7 = (bf16[256,256]{1,0:T(8,128)(2,1)S(1)}, bf16[256,256]{1,0:T(8,128)(2,1)}, u32[]{:S(2)}) copy-start(bf16[256,256]{1,0:T(8,128)(2,1)} %wv_ref.2) | copy-start | bytes 393220
  18.1 2.4 %copy-start.8 = (bf16[256,256]{1,0:T(8,128)(2,1)S(1)}, bf16[256,256]{1,0:T(8,128)(2,1)}, u32[]{:S(2)}) copy-start(bf16[256,256]{1,0:T(8,128)(2,1)} %wo_ref.2) | copy-start | bytes 393220
  18.1 2.4 %copy-start.14 = (f32[256]{0:T(256)S(1)}, f32[256]{0:T(256)}, u32[]{:S(2)}) copy-start(f32[256]{0:T(256)} %param.28) | copy-start | bytes 3076
  18.1 2.4 %copy-start.15 = (f32[256]{0:T(256)S(1)}, f32[256]{0:T(256)}, u32[]{:S(2)}) copy-start(f32[256]{0:T(256)} %param.35) | copy-start | bytes 3076
  18.2 2.4 %copy-start.17 = (f32[8]{0:T(128)S(1)}, f32[8]{0:T(128)}, u32[]{:S(2)}) copy-start(f32[8]{0:T(128)} %param.27) | copy-start | bytes 100
  18.2 2.4 %copy-start.18 = (f32[8]{0:T(128)S(1)}, f32[8]{0:T(128)}, u32[]{:S(2)}) copy-start(f32[8]{0:T(128)} %param.33) | copy-start | bytes 100
  18.2 2.4 %copy-start.19 = (f32[8]{0:T(128)S(1)}, f32[8]{0:T(128)}, u32[]{:S(2)}) copy-start(f32[8]{0:T(128)} %param.34) | copy-start | bytes 100
  20.5 0.7 copy-start.13
  20.5 0.7 copy-start.16
  21.2 33.5 %copy-start.1 = (bf16[256,1024]{1,0:T(8,128)(2,1)S(1)}, bf16[256,1024]{1,0:T(8,128)(2,1)}, u32[]{:S(2)}) copy-start(bf16[256,1024]{1,0:T(8,128)(2,1)} %wu_ref.1) | copy-start | bytes 1572868
  21.2 33.5 %copy-start.2 = (bf16[1024,256]{1,0:T(8,128)(2,1)S(1)}, bf16[1024,256]{1,0:T(8,128)(2,1)}, u32[]{:S(2)}) copy-start(bf16[1024,256]{1,0:T(8,128)(2,1)} %wd_ref.1) | copy-start | bytes 1572868
  21.2 33.5 %copy-start.9 = (bf16[256,256]{1,0:T(8,128)(2,1)S(1)}, bf16[256,256]{1,0:T(8,128)(2,1)}, u32[]{:S(2)}) copy-start(bf16[256,256]{1,0:T(8,128)(2,1)} %wq_ref.3) | copy-start | bytes 393220
  21.2 33.5 %copy-start.10 = (bf16[256,256]{1,0:T(8,128)(2,1)S(1)}, bf16[256,256]{1,0:T(8,128)(2,1)}, u32[]{:S(2)}) copy-start(bf16[256,256]{1,0:T(8,128)(2,1)} %wk_ref.3) | copy-start | bytes 393220
  24.9 29.8 %copy-start = (bf16[256,1024]{1,0:T(8,128)(2,1)S(1)}, bf16[256,1024]{1,0:T(8,128)(2,1)}, u32[]{:S(2)}) copy-start(bf16[256,1024]{1,0:T(8,128)(2,1)} %wg_ref.1) | copy-start | bytes 1572868

commit v8 on v7

--- a/solution.py
+++ b/solution.py
@@ -31,11 +31,6 @@
     at = [lax.broadcasted_iota(jnp.int32, (HEADS, HEADS), axis) for axis in range(2)]
     picked = jnp.where(at[0] == at[1], jnp.broadcast_to(ref[...], (HEADS, HEADS)), 0.0)
     return jnp.broadcast_to(jnp.sum(picked, axis=1, keepdims=True), (HEADS, D))
-
-
-def twice_kernel(x_ref, out_ref):
-    for j in range(XA):
-        out_ref[j] = x_ref[...]
 
 
 def row_kernel(
@@ -198,13 +193,7 @@
     norm_lat, query_lat, key_lat, value_lat, out_lat, temp_lat, bias_lat, norm_mlp, w_gate, w_up, w_down,
 ):
     keyf = key_features()
-    twice = pl.pallas_call(
-        twice_kernel,
-        out_shape=jax.ShapeDtypeStruct((XA, 8, 32, D), BF16),
-        in_specs=[VMEM],
-        out_specs=VMEM,
-        compiler_params=PARAMS,
-    )(fields)
+    twice = jnp.concatenate([fields] * XA, axis=0)
     half = lax.all_to_all(twice.reshape(16, 32, D), ("xa", "yl", "xb"), split_axis=0, concat_axis=0, tiled=True)
     row = lax.all_gather(half, "c", axis=0, tiled=True)
     row = row.reshape(1024, D)

time: 70.4 us -> 70.5 us (level)
  other arithmetic: 0 us -> 1 us
  local copies, waits for them, and re-layouts: 1.58 us -> 0.68 us
    concatenate x0 -> x1, other arithmetic: none -> 1 us  [body(): twice = jnp.concatenate([fields] * XA, axis=0)]
    unnamed x40 -> x38, local copies, waits for them, and re-layouts: 1.58 us -> 0.68 us
where the time goes in v8:
time: 70.5 us; the launch traced here: 70.3 us
  blocking collectives  61.7 us (88%)
  Pallas kernels  6.63 us (9%)
  other arithmetic  1 us (1%)
    all_to_all x1, blocking collectives, body(): lax.all_to_all(sent.reshape(128, 8, 128), ('yh', 'z', 'yl', 'xb'), split_...  29.8 us
    all_to_all x1, blocking collectives, body(): lax.all_to_all(twice.reshape(16, 32, D), ('xa', 'yl', 'xb'), split_axis=0...  17.2 us
    all_to_all x1, blocking collectives, body(): lax.all_to_all(done.reshape(8, 32, D), 'z', split_axis=0, concat_axis=0,...  12.5 us
    pallas_call x1, Pallas kernels, body(): pl.pallas_call(row_kernel, out_shape=(jax.ShapeDtypeStruct((2, 512, 128),...  3.65 us
    all_gather x1, blocking collectives, body(): row = lax.all_gather(half, 'c', axis=0, tiled=True)  2.31 us
    pallas_call x1, Pallas kernels, body(): pl.pallas_call(col_kernel, out_shape=jax.ShapeDtypeStruct((8, 4, 8, D), B...  2.13 us

profile of v8, /device:TPU:2, one launch (start us, length us, event | category | flops | bytes accessed | tf_op | source)
XLA Modules:
  0.0 70.3 jit_solution(6795541231944202186)
XLA Ops:
  0.0 1.0 %pad_maximum_fusion = bf16[16,32,256]{2,1,0:T(8,128)(2,1)S(1)} fusion(bf16[8,32,256]{2,1,0:T(8,128)(2,1)} %param.20), kind=kLoop, calls=%fused_computation | loop fusion | flops 131072 | bytes 393216 | tf_op jit(solution)/shard_map/concatenate | solution.py:196
  1.0 0.0 copy-start.10
  1.0 0.0 copy-start.11
  1.0 17.2 %all_to_all.15 = bf16[16,32,256]{2,1,0:T(8,128)(2,1)S(1)} all-to-all(bf16[16,32,256]{2,1,0:T(8,128)(2,1)S(1)} %pad_maximum_fusion), channel_id=1, replica_groups=mesh['yl'=4,'xa'=2,'xb'=2,'c'=2,'z'=8,'yh'=2] {'xa','yl','xb'}, dimensions={0} | all-to-all | bytes 524288 | tf_op jit(solution)/shard_map/all_to_all | solution.py:197
  18.2 0.0 copy-start.3
  18.2 0.0 copy-start.4
  18.2 0.0 copy-start.5
  18.2 0.0 copy-start.6
  18.2 0.0 copy-start.7
  18.2 0.0 copy-start.13
  18.2 0.0 copy-start.14
  18.2 0.0 copy-start.16
  18.3 0.0 copy-start.17
  18.3 0.0 copy-start.18
  18.3 2.3 %all_gather.3 = bf16[32,32,256]{2,1,0:T(8,128)(2,1)S(1)} all-gather(bf16[16,32,256]{2,1,0:T(8,128)(2,1)S(1)} %all_to_all.15), channel_id=1, replica_groups=mesh['yl'=4,'xa'=2,'xb'=2,'c'=2,'z'=8,'yh'=2] {'c'}, dimensions={0}, use_global_device_ids=true | all-gather | bytes 786432 | tf_op jit(solution)/shard_map/all_gather | solution.py:198
  20.6 0.0 copy-start.12
  20.6 0.0 copy-start.15
  20.6 0.0 copy-done.3
  20.6 0.0 copy-done.4
  20.6 0.0 copy-done.5
  20.6 0.0 copy-done.6
  20.6 0.0 copy-done.7
  20.6 0.0 copy-done.13
  20.6 0.0 copy-done.14
  20.7 0.0 copy-done.16
  20.7 0.0 copy-done.17
  20.7 0.0 copy-done.18
  20.7 0.6 copy-done.12
  21.3 0.0 copy-done.15
  21.3 0.0 copy-start.1
  21.3 0.0 copy-start.2
  21.3 0.0 copy-start.8
  21.3 0.0 copy-start.9
  21.3 3.7 %shard_map.190 = (bf16[2,512,128]{2,1,0:T(8,128)(2,1)S(1)}, f32[18,256]{1,0:T(8,128)S(1)}) custom-call(bf16[1024,256]{1,0:T(8,128)(2,1)S(1)} %bitcast.12, f32[1,256]{1,0:T(1,128)S(1)} %bitcast.17, f32[1,256]{1,0:T(1,128)S(1)} %bitcast.18, f32[1,256]{1,0:T(1,128)S(1)} %bitcast.19, f32[1,8]{1,0:T(1,128)S(1)} %bitcast.20, f32[1,8]{1,0:T(1,128)S(1)} %bitcast.21, ...), custom_call_target="tpu_custom_call" | custom-call | tf_op jit(solution)/shard_map/pallas_call | solution.py:200
  25.0 0.0 copy-start
  25.0 29.8 %all_to_all.16 = bf16[128,8,128]{2,1,0:T(8,128)(2,1)S(1)} all-to-all(bf16[128,8,128]{2,1,0:T(8,128)(2,1)S(1)} %bitcast.16), channel_id=1, replica_groups=mesh['yl'=4,'xa'=2,'xb'=2,'c'=2,'z'=8,'yh'=2] {'yh','z','yl','xb'}, dimensions={0} | all-to-all | bytes 524288 | tf_op jit(solution)/shard_map/all_to_all | solution.py:218
  54.7 0.0 copy-done.10
  54.7 0.0 copy-done.11
  54.7 0.0 copy-done.1
  54.7 0.0 copy-done.2
  54.7 0.0 copy-done.8
  54.8 0.0 copy-done.9
  54.8 0.0 copy-done
  54.8 2.1 %shard_map.191 = bf16[8,4,8,256]{3,2,1,0:T(8,128)(2,1)S(1)} custom-call(bf16[1024,128]{1,0:T(8,128)(2,1)S(1)} %bitcast.13, f32[18,256]{1,0:T(8,128)S(1)} %get-tuple-element.8.table_ref, bf16[256,256]{1,0:T(8,128)(2,1)S(1)} %copy-done.8, bf16[256,256]{1,0:T(8,128)(2,1)S(1)} %copy-done.9, bf16[256,256]{1,0:T(8,128)(2,1)S(1)} %copy-done.10, ...), custom_call_target="tpu_custom_call" | custom-call | tf_op jit(solution)/shard_map/pallas_call | solution.py:221
  56.9 12.5 %all_to_all.17 = bf16[8,32,256]{2,1,0:T(8,128)(2,1)S(1)} all-to-all(bf16[8,32,256]{2,1,0:T(8,128)(2,1)S(1)} %bitcast.14), channel_id=1, replica_groups=mesh['yl'=4,'xa'=2,'xb'=2,'c'=2,'z'=8,'yh'=2] {'z'}, dimensions={0} | all-to-all | bytes 262144 | tf_op jit(solution)/shard_map/all_to_all | solution.py:235
  69.4 0.8 %shard_map.192 = bf16[8,32,256]{2,1,0:T(8,128)(2,1)} custom-call(bf16[256,256]{1,0:T(8,128)(2,1)S(1)} %bitcast.15), custom_call_target="tpu_custom_call" | custom-call | tf_op jit(solution)/shard_map/pallas_call | solution.py:236
Async XLA Ops:
  1.0 53.7 %copy-start.10 = (bf16[256,256]{1,0:T(8,128)(2,1)S(1)}, bf16[256,256]{1,0:T(8,128)(2,1)}, u32[]{:S(2)}) copy-start(bf16[256,256]{1,0:T(8,128)(2,1)} %wv_ref.3) | copy-start | bytes 393220
  1.0 53.7 %copy-start.11 = (bf16[256,256]{1,0:T(8,128)(2,1)S(1)}, bf16[256,256]{1,0:T(8,128)(2,1)}, u32[]{:S(2)}) copy-start(bf16[256,256]{1,0:T(8,128)(2,1)} %wo_ref.3) | copy-start | bytes 393220
  18.2 2.4 %copy-start.3 = (bf16[1024,128]{1,0:T(8,128)(2,1)S(1)}, bf16[1024,128]{1,0:T(8,128)(2,1)}, u32[]{:S(2)}) copy-start(bf16[1024,128]{1,0:T(8,128)(2,1)} %constant.2.clone.keyf_ref) | copy-start | bytes 786436
  18.2 2.4 %copy-start.4 = (bf16[256,256]{1,0:T(8,128)(2,1)S(1)}, bf16[256,256]{1,0:T(8,128)(2,1)}, u32[]{:S(2)}) copy-start(bf16[256,256]{1,0:T(8,128)(2,1)} %wq_ref.2) | copy-start | bytes 393220
  18.2 2.4 %copy-start.5 = (bf16[256,256]{1,0:T(8,128)(2,1)S(1)}, bf16[256,256]{1,0:T(8,128)(2,1)}, u32[]{:S(2)}) copy-start(bf16[256,256]{1,0:T(8,128)(2,1)} %wk_ref.2) | copy-start | bytes 393220
  18.2 2.4 %copy-start.6 = (bf16[256,256]{1,0:T(8,128)(2,1)S(1)}, bf16[256,256]{1,0:T(8,128)(2,1)}, u32[]{:S(2)}) copy-start(bf16[256,256]{1,0:T(8,128)(2,1)} %wv_ref.2) | copy-start | bytes 393220
  18.2 2.4 %copy-start.7 = (bf16[256,256]{1,0:T(8,128)(2,1)S(1)}, bf16[256,256]{1,0:T(8,128)(2,1)}, u32[]{:S(2)}) copy-start(bf16[256,256]{1,0:T(8,128)(2,1)} %wo_ref.2) | copy-start | bytes 393220
  18.2 2.4 %copy-start.13 = (f32[256]{0:T(256)S(1)}, f32[256]{0:T(256)}, u32[]{:S(2)}) copy-start(f32[256]{0:T(256)} %param.28) | copy-start | bytes 3076
  18.2 2.4 %copy-start.14 = (f32[256]{0:T(256)S(1)}, f32[256]{0:T(256)}, u32[]{:S(2)}) copy-start(f32[256]{0:T(256)} %param.35) | copy-start | bytes 3076
  18.2 2.4 %copy-start.16 = (f32[8]{0:T(128)S(1)}, f32[8]{0:T(128)}, u32[]{:S(2)}) copy-start(f32[8]{0:T(128)} %param.27) | copy-start | bytes 100
  18.3 2.4 %copy-start.17 = (f32[8]{0:T(128)S(1)}, f32[8]{0:T(128)}, u32[]{:S(2)}) copy-start(f32[8]{0:T(128)} %param.33) | copy-start | bytes 100
  18.3 2.4 %copy-start.18 = (f32[8]{0:T(128)S(1)}, f32[8]{0:T(128)}, u32[]{:S(2)}) copy-start(f32[8]{0:T(128)} %param.34) | copy-start | bytes 100
  20.6 0.7 copy-start.12
  20.6 0.7 copy-start.15
  21.3 33.5 %copy-start.1 = (bf16[256,1024]{1,0:T(8,128)(2,1)S(1)}, bf16[256,1024]{1,0:T(8,128)(2,1)}, u32[]{:S(2)}) copy-start(bf16[256,1024]{1,0:T(8,128)(2,1)} %wu_ref.1) | copy-start | bytes 1572868
  21.3 33.5 %copy-start.2 = (bf16[1024,256]{1,0:T(8,128)(2,1)S(1)}, bf16[1024,256]{1,0:T(8,128)(2,1)}, u32[]{:S(2)}) copy-start(bf16[1024,256]{1,0:T(8,128)(2,1)} %wd_ref.1) | copy-start | bytes 1572868
  21.3 33.5 %copy-start.8 = (bf16[256,256]{1,0:T(8,128)(2,1)S(1)}, bf16[256,256]{1,0:T(8,128)(2,1)}, u32[]{:S(2)}) copy-start(bf16[256,256]{1,0:T(8,128)(2,1)} %wq_ref.3) | copy-start | bytes 393220
  21.3 33.5 %copy-start.9 = (bf16[256,256]{1,0:T(8,128)(2,1)S(1)}, bf16[256,256]{1,0:T(8,128)(2,1)}, u32[]{:S(2)}) copy-start(bf16[256,256]{1,0:T(8,128)(2,1)} %wk_ref.3) | copy-start | bytes 393220
  25.0 29.8 %copy-start = (bf16[256,1024]{1,0:T(8,128)(2,1)S(1)}, bf16[256,1024]{1,0:T(8,128)(2,1)}, u32[]{:S(2)}) copy-start(bf16[256,1024]{1,0:T(8,128)(2,1)} %wg_ref.1) | copy-start | bytes 1572868
